TPU v7x, 32 devices: a whole 2x2x4 slice. The times are simulated.
32 devices in a mesh: block: 8 (over z, y), dp: 4 (over x, core).
Axes of the slice: x: 2, y: 2, z: 4, core: 2. Of those that a mesh axis runs over, the one named last changes fastest.
Arguments:
- mixture: float32 [32, 9600], P('dp', 'block'), may hold values from -6 to 6
- target: float32 [32, 9600], P('dp', 'block'), may hold values from -6 to 6
- lengths: int32 [32], P('dp'), may hold values from 1200 to 9600, as said below
- input_gates: float32 [4, 2, 64, 512], replicated, may hold values from -0.75 to 0.75
- recur_gates: float32 [4, 2, 128, 512], replicated, may hold values from -0.5 to 0.5
- projections: float32 [1184, 64], replicated
- vectors: float32 [5120], replicated
- moment_input: float32 [4, 2, 64, 512], replicated, may hold values from -7.1525574e-07 to 7.1525574e-07
- moment_recur: float32 [4, 2, 128, 512], replicated, may hold values from -7.1525574e-07 to 7.1525574e-07
- moment_proj: float32 [1184, 64], replicated, may hold values from -7.1525574e-07 to 7.1525574e-07
- moment_vecs: float32 [5120], replicated, may hold values from -1.9073486e-06 to 1.9073486e-06
- square_input: float32 [4, 2, 64, 512], replicated, may hold values from 1.1529663e-15 to 4.6118653e-15
- square_recur: float32 [4, 2, 128, 512], replicated, may hold values from 1.1529663e-15 to 4.6118653e-15
- square_proj: float32 [1184, 64], replicated, may hold values from 1.1529663e-15 to 4.6118653e-15
- square_vecs: float32 [5120], replicated, may hold values from 1.0376697e-14 to 4.150679e-14
- average_input: float32 [4, 2, 64, 512], replicated, may hold values from -0.3125 to 0.3125
- average_recur: float32 [4, 2, 128, 512], replicated, may hold values from -0.3125 to 0.3125
- average_proj: float32 [1184, 64], replicated, may hold values from -0.3125 to 0.3125
- average_vecs: float32 [5120], replicated, may hold values from -1.75 to 1.75
Outputs:
- loss_sum: float32 [], replicated
- valid_count: float32 [], replicated
- grad_norm: float32 [], replicated
- moments_input: float32 [4, 2, 64, 512], replicated
- moments_recur: float32 [4, 2, 128, 512], replicated
- moments_proj: float32 [1184, 64], replicated
- moments_vecs: float32 [5120], replicated
- squares_input: float32 [4, 2, 64, 512], replicated
- squares_recur: float32 [4, 2, 128, 512], replicated
- squares_proj: float32 [1184, 64], replicated
- squares_vecs: float32 [5120], replicated
- master_input: float32 [4, 2, 64, 512], replicated
- master_recur: float32 [4, 2, 128, 512], replicated
- master_proj: float32 [1184, 64], replicated
- master_vecs: float32 [5120], replicated
- smooth_input: float32 [4, 2, 64, 512], replicated
- smooth_recur: float32 [4, 2, 128, 512], replicated
- smooth_proj: float32 [1184, 64], replicated
- smooth_vecs: float32 [5120], replicated
- lowcopy_input: bfloat16 [4, 2, 64, 512], replicated
- lowcopy_recur: bfloat16 [4, 2, 128, 512], replicated
- lowcopy_proj: bfloat16 [1184, 64], replicated
- lowcopy_vecs: bfloat16 [5120], replicated
Inputs may be any that keep to these rules, and one draw needn't show every extreme that they name: `lengths`: in each aligned group of 8 mixtures (one index of dp) one mixture, which one drawn from the seed, has length 9600.
All inputs are finite; a program needn't handle non-finite values.
Results may differ from a plain program's by a relative error of at most 0.0015.
The roundings to bfloat16 on the way count: a program that leaves them out, or rounds other values in their place, can miss the bound.
Values may be sent and summed in bfloat16 or wider, within the bound.
No kernel may reach another device: no remote copies, remote signals or barrier semaphores. Data moves between devices by JAX's collectives and lax.ppermute only.
A program may use at most 384 MiB of HBM per device.

v0:
```python
import functools

import jax
import jax.numpy as jnp
from jax import lax
from jax.experimental import pallas as pl
from jax.experimental.pallas import tpu as pltpu
from jax.sharding import PartitionSpec as P

N = 64
B = 64
H = 128
K = 100
STRIDE = 8
LAYERS = 2
STEP = 10
HOP = 50
TILES = 3
M = 8
FRAMES = 150
BASE = 4 * LAYERS * H
PERIOD = 8 * H + 3 * B
ROWS_G = 424
BLOCKS = 208
PADDED = 216
CHUNK = 416

EPS_NORM = 1e-05
CLIP = 0.001
RATE = 0.1
BETA_ONE = 0.9
BETA_TWO = 0.999
ADAM_EPS = 1e-08
DECAY = 0.01
KEEP = 0.9

BF = jnp.bfloat16
F32 = jnp.float32
SDS = jax.ShapeDtypeStruct


def dot(left, right):
    return jnp.dot(left, right, preferred_element_type=F32)


def dot_rows(left, right):
    return lax.dot_general(left, right, (((0,), (0,)), ((), ())), preferred_element_type=F32)


def half_scale():
    lane = lax.broadcasted_iota(jnp.int32, (1, 4 * H), 1)
    return jnp.where((lane >= 2 * H) & (lane < 3 * H), 1.0, 0.5)


def gate_acts(z):
    act = jnp.tanh(z)
    sig_i = 0.5 * act[:, :H] + 0.5
    sig_f = 0.5 * act[:, H : 2 * H] + 0.5
    sig_o = 0.5 * act[:, 3 * H :] + 0.5
    return sig_i, sig_f, act[:, 2 * H : 3 * H], sig_o


def norm_parts(value):
    center = value - jnp.mean(value, -1, keepdims=True)
    spread = jnp.mean(center * center, -1, keepdims=True)
    scale = lax.rsqrt(spread + EPS_NORM)
    return center * scale, scale


def norm_back(grad, unit, scale, gain):
    inner = grad * gain
    return scale * (
        inner
        - jnp.mean(inner, -1, keepdims=True)
        - unit * jnp.mean(inner * unit, -1, keepdims=True)
    )


def live(lim, start, count):
    pos = lax.broadcasted_iota(jnp.int32, (count, M, B), 0) + start
    return jnp.where(pos * STRIDE < lim[None], 1.0, 0.0).reshape(count * M, B)


def own(start, count):
    pos = lax.broadcasted_iota(jnp.int32, (count, M, B), 0) + start
    return jnp.where(pos < FRAMES, 1.0, 0.0).reshape(count * M, B)


def chunk_of(steps, rows):
    best = 1
    for size in range(1, steps + 1):
        if steps % size == 0 and size * rows <= 512 and size * rows % 16 == 0:
            best = size
    return best


class Shape:
    def __init__(self, groups, steps, rows):
        self.groups, self.steps, self.rows = groups, steps, rows
        self.size = steps * rows
        self.chunk = chunk_of(steps, rows)
        self.crows = self.chunk * rows
        self.chunks = steps // self.chunk
        self.wide = (steps + 2) * rows
        self.unroll = 4 if steps % 4 == 0 else 1


def chunk_loop(shape, fn):
    for g in range(shape.groups):

        def step(i, _, g=g):
            fn(g, i, pl.multiple_of(i * shape.crows, 8))
            return 0

        lax.fori_loop(0, shape.chunks, step, 0)


def forward_weights(gi, gr, wi, wr):
    half = half_scale()
    for d in range(2):
        wi[d] = (gi[0, d].astype(BF).astype(F32) * half).astype(BF)
        wr[d] = (gr[0, d].astype(BF).astype(F32) * half).astype(BF)


def lstm_scan(shape, pg, wr, h_ref, c_ref):
    G, S, R = shape.groups, shape.steps, shape.rows
    pad = jnp.zeros((R, 2 * H), F32)
    for g in range(G):
        for ref in (h_ref, c_ref):
            ref[g, :R] = pad
            ref[g, (S + 1) * R :] = pad

    def one(d, t, hidden, memory):
        at = pl.multiple_of(t * R, 8)
        pre = jnp.concatenate([pg[d, g, pl.ds(at, R), :] for g in range(G)], 0)
        z = pre + dot(hidden, wr[d])
        sig_i, sig_f, tan_g, sig_o = gate_acts(z)
        memory = sig_f * memory + sig_i * tan_g
        hidden = (sig_o * jnp.tanh(memory)).astype(BF)
        full = hidden.astype(F32)
        after = pl.multiple_of(t * R + R, 8)
        for g in range(G):
            h_ref[g, pl.ds(after, R), d * H : (d + 1) * H] = full[g * R : (g + 1) * R]
            c_ref[g, pl.ds(after, R), d * H : (d + 1) * H] = memory[g * R : (g + 1) * R]
        return hidden, memory

    def step(s, carry):
        hf, cf, hb, cb = carry
        hf, cf = one(0, s, hf, cf)
        hb, cb = one(1, S - 1 - s, hb, cb)
        return hf, cf, hb, cb

    zero = jnp.zeros((G * R, H), F32)
    start = (zero.astype(BF), zero, zero.astype(BF), zero)
    lax.fori_loop(0, S, step, start, unroll=shape.unroll)


def lstm_scan_back(shape, z, dh, c_ref, wrt):
    G, S, R = shape.groups, shape.steps, shape.rows

    def one(d, t, rec_hidden, rec_memory):
        def take(ref, at, lanes):
            at = pl.multiple_of(at, 8)
            return jnp.concatenate([ref[g, pl.ds(at, R), lanes] for g in range(G)], 0)

        lanes = slice(d * H, (d + 1) * H)
        at = pl.multiple_of(t * R, 8)
        zt = jnp.concatenate([z[d, g, pl.ds(at, R), :] for g in range(G)], 0)
        sig_i, sig_f, tan_g, sig_o = gate_acts(zt)
        tan_c = jnp.tanh(take(c_ref, t * R + R, lanes))
        before = take(c_ref, t * R + 2 * R * d, lanes)
        grad_h = take(dh, t * R, lanes) + rec_hidden
        grad_c = rec_memory + grad_h * (sig_o * (1.0 - tan_c * tan_c))
        grad_pre = jnp.concatenate(
            [
                grad_c * (tan_g * sig_i * (1.0 - sig_i)),
                grad_c * (before * sig_f * (1.0 - sig_f)),
                grad_c * (sig_i * (1.0 - tan_g * tan_g)),
                grad_h * (tan_c * sig_o * (1.0 - sig_o)),
            ],
            -1,
        ).astype(BF)
        full = grad_pre.astype(F32)
        for g in range(G):
            z[d, g, pl.ds(at, R), :] = full[g * R : (g + 1) * R]
        return dot(grad_pre, wrt[d]), grad_c * sig_f

    def step(s, carry):
        hf, cf, hb, cb = carry
        hf, cf = one(0, S - 1 - s, hf, cf)
        hb, cb = one(1, s, hb, cb)
        return hf, cf, hb, cb

    zero = jnp.zeros((G * R, H), F32)
    lax.fori_loop(0, S, step, (zero,) * 4, unroll=shape.unroll)


def branch_pregates(shape, xs, wi, bias, pg):
    half = half_scale()

    def fill(g, i, r0):
        x = xs[g, pl.ds(r0, shape.crows), :].astype(BF)
        for d in range(2):
            pg[d, g, pl.ds(r0, shape.crows), :] = dot(x, wi[d]) + bias[0, d : d + 1] * half

    chunk_loop(shape, fill)


def branch_back(shape, grads, xs, h_ref, c_ref, weights, bias, others, wout, out, scratch):
    gi, gr = weights
    wi, wr, wit, wrt, wo, wot, z, dh = scratch
    n, R = shape.crows, shape.rows
    forward_weights(gi, gr, wi, wr)
    for d in range(2):
        wit[d] = jnp.transpose(gi[0, d]).astype(BF)
        wrt[d] = jnp.transpose(gr[0, d]).astype(BF)
    wo[...] = wout.astype(BF)
    wot[...] = jnp.transpose(wout).astype(BF)
    out[...] = jnp.zeros_like(out)
    half = half_scale()
    o_bias, gain = others[0, 0:1], others[0, 1:2]

    def first(g, i, r0):
        now = h_ref[g, pl.ds(pl.multiple_of(r0 + R, 8), n), :].astype(BF)
        unit, scale = norm_parts(dot(now, wo[...]) + o_bias)
        grad = grads(g, i, r0)
        low = norm_back(grad, unit, scale, gain).astype(BF)
        dh[g, pl.ds(r0, n), :] = dot(low, wot[...])
        turned = dot_rows(low, now)
        out[384:416] += jnp.concatenate([turned[:32], turned[32:]], 1)
        for row, value in ((418, low.astype(F32)), (419, grad * unit), (420, grad)):
            out[row : row + 1, :B] += jnp.sum(value, 0, keepdims=True)
        x = xs[g, pl.ds(r0, n), :].astype(BF)
        for d in range(2):
            before = h_ref[
                g, pl.ds(pl.multiple_of(r0 + 2 * R * d, 8), n), d * H : (d + 1) * H
            ].astype(BF)
            z[d, g, pl.ds(r0, n), :] = dot(before, wr[d]) + dot(x, wi[d]) + bias[0, d : d + 1] * half

    chunk_loop(shape, first)
    lstm_scan_back(shape, z, dh, c_ref, wrt)

    def last(use):
        def fn(g, i, r0):
            x = xs[g, pl.ds(r0, n), :].astype(BF)
            total = None
            for d in range(2):
                full = z[d, g, pl.ds(r0, n), :]
                low = full.astype(BF)
                before = h_ref[
                    g, pl.ds(pl.multiple_of(r0 + 2 * R * d, 8), n), d * H : (d + 1) * H
                ].astype(BF)
                out[d * B : (d + 1) * B] += dot_rows(x, low)
                out[128 + d * H : 128 + (d + 1) * H] += dot_rows(before, low)
                out[416 + d : 417 + d] += jnp.sum(full, 0, keepdims=True)
                part = dot(low, wit[d])
                total = part if total is None else total + part
            use(g, i, r0, total)

        chunk_loop(shape, fn)

    return last


def back_scratch(shape):
    return [
        pltpu.VMEM((2, B, 4 * H), BF),
        pltpu.VMEM((2, H, 4 * H), BF),
        pltpu.VMEM((2, 4 * H, B), BF),
        pltpu.VMEM((2, 4 * H, H), BF),
        pltpu.VMEM((2 * H, B), BF),
        pltpu.VMEM((B, 2 * H), BF),
        pltpu.VMEM((2, shape.groups, shape.size, 4 * H), F32),
        pltpu.VMEM((shape.groups, shape.size, 2 * H), F32),
    ]


def send_tiles(res, send, nb, RI):
    for d in range(nb):
        for c in range(TILES):
            send[d, c] = res[c, d * RI : (d + 1) * RI].astype(BF)


def add_tiles(res, back, nb, RI, lim, pads):
    for d in range(nb):
        for c in range(TILES):
            lo, hi = d * RI, min((d + 1) * RI, K * M)
            if lo >= hi:
                continue
            value = back[d, c].astype(F32)[: hi - lo]
            mask = live(lim, c * HOP + lo // M, (hi - lo) // M)
            res[c, lo:hi] = (res[c, lo:hi] + value) * mask
    del pads


def windows_of(mix, win):
    for i in range(BLOCKS):
        win[i * M : (i + 1) * M] = mix[:, STRIDE * i : STRIDE * (i + 2)]


def proj_rows(proj, start, count):
    return proj[start : start + count]


def intra_forward(shape, res, lim, gi, gr, bias, others, wout, x_out, h_out, c_out, scratch):
    wi, wr, pg = scratch
    forward_weights(gi, gr, wi, wr)
    n = shape.crows

    def keep(g, i, r0):
        x_out[g, pl.ds(pl.multiple_of(r0, 16), n), :] = res[g, pl.ds(r0, n), :].astype(BF)

    chunk_loop(shape, keep)
    branch_pregates(shape, res, wi, bias, pg)
    lstm_scan(shape, pg, wr, h_out, c_out)
    low_out = wout.astype(BF)
    o_bias, gain, beta = others[0, 0:1], others[0, 1:2], others[0, 2:3]

    def close(g, i, r0):
        now = h_out[g, pl.ds(pl.multiple_of(r0 + shape.rows, 8), n), :].astype(BF)
        unit, _ = norm_parts(dot(now, low_out) + o_bias)
        mask = live(lim[...], g * HOP + i * shape.chunk, shape.chunk)
        res[g, pl.ds(r0, n), :] = (res[g, pl.ds(r0, n), :] + (unit * gain + beta)) * mask

    chunk_loop(shape, close)


def first_kernel(shape, nb, RI, mix, lim, proj, vec, gi, gr, bias, others, res, send, x_out, h_out, c_out, win, wi, wr, pg, flat, bottle):
    windows_of(mix, flat)
    win[...] = flat[...].astype(BF)
    w_enc = proj_rows(proj, BASE + N + B, 2 * STRIDE).astype(BF)
    w_bn = proj_rows(proj, BASE, N).astype(BF)
    gain, beta, b_bias = vec[0:1], vec[1:2], vec[2:3]
    for i in range(BLOCKS * M // CHUNK):
        at = i * CHUNK
        pre = dot(win[at : at + CHUNK], w_enc)
        unit, _ = norm_parts(softplus(pre))
        normed = (unit * gain + beta).astype(BF)
        mask = live(lim[...], i * (CHUNK // M) - 1, CHUNK // M)
        bottle[at : at + CHUNK] = (dot(normed, w_bn) + b_bias) * mask
    for c in range(TILES):
        res[c, : K * M] = bottle[(c * HOP + 1) * M : (c * HOP + 1 + K) * M]
        if nb * RI > K * M:
            res[c, K * M :] = jnp.zeros((nb * RI - K * M, B), F32)
    wout = proj_rows(proj, 0, 2 * H)
    intra_forward(shape, res, lim, gi, gr, bias, others, wout, x_out, h_out, c_out, (wi, wr, pg))
    send_tiles(res, send, nb, RI)


def softplus(value):
    return jnp.maximum(value, 0.0) + jnp.log1p(jnp.exp(-jnp.abs(value)))


def third_kernel(shape, nb, RI, index, res_in, back, lim, proj, gi, gr, bias, others, res, send, x_out, h_out, c_out, wi, wr, pg):
    res[...] = res_in[...]
    add_tiles(res, back, nb, RI, lim[...], None)
    wout = proj_rows(proj, index * 2 * H, 2 * H)
    intra_forward(shape, res, lim, gi, gr, bias, others, wout, x_out, h_out, c_out, (wi, wr, pg))
    send_tiles(res, send, nb, RI)


def inter_kernel(shape, RI, index, rows, proj, gi, gr, bias, others, normed, h_out, c_out, wi, wr, pg, xs):
    T = shape.steps
    forward_weights(gi, gr, wi, wr)

    def widen(t, _):
        xs[0, pl.ds(pl.multiple_of(t * RI, 8), RI), :] = rows[t].astype(F32)
        return 0

    lax.fori_loop(0, T, widen, 0)
    branch_pregates(shape, xs, wi, bias, pg)
    lstm_scan(shape, pg, wr, h_out, c_out)
    low_out = proj_rows(proj, index * 2 * H, 2 * H).astype(BF)
    o_bias, gain, beta = others[0, 0:1], others[0, 1:2], others[0, 2:3]

    def close(g, i, r0):
        now = h_out[g, pl.ds(pl.multiple_of(r0 + RI, 8), shape.crows), :].astype(BF)
        unit, _ = norm_parts(dot(now, low_out) + o_bias)
        value = unit * gain + beta
        for j in range(shape.chunk):
            normed[i * shape.chunk + j] = value[j * RI : (j + 1) * RI].astype(BF)

    chunk_loop(shape, close)


def part_kernel(nb, RI, res_in, back, lim, part, up, down, res):
    res[...] = res_in[...]
    add_tiles(res, back, nb, RI, lim[...], None)
    half = HOP * M
    part[:half] = res[0, :half]
    for c in range(1, TILES):
        part[c * half : (c + 1) * half] = res[c, :half] + res[c - 1, half : 2 * half]
    part[TILES * half :] = res[TILES - 1, half : 2 * half]
    up[...] = part[TILES * half - M :]
    down[...] = part[: half + M]


def middle_kernel(nb, RI, part, before, after, lim, edge, win, goal, proj, vec, send, gres, genc, gm, feats, dec, tgt, gest, enc, gate, src, act):
    half = HOP * M
    top = M + TILES * half
    feats[...] = jnp.zeros_like(feats)
    feats[:M] = before[:M]
    feats[M : M + half] = part[:half] + before[M:]
    feats[M + half : top] = part[half : TILES * half]
    feats[top : top + half] = part[TILES * half :] + after[:half]
    feats[top + half : top + half + M] = after[half:]
    w_mask = proj_rows(proj, BASE + N, B)
    w_enc = proj_rows(proj, BASE + N + B, 2 * STRIDE).astype(BF)
    w_dec = proj_rows(proj, BASE + N + B + 2 * STRIDE, 2 * STRIDE)
    low_mask = w_mask.astype(BF)
    turned_mask = jnp.transpose(w_mask).astype(BF)
    low_dec = w_dec.astype(BF)
    m_bias = vec[3:4]
    root = 0.7978845608028654
    cube = 0.044715
    total = BLOCKS * M
    dec[total:] = jnp.zeros((PADDED * M - total, 2 * STRIDE), F32)
    for i in range(total // CHUNK):
        rows = slice(i * CHUNK, (i + 1) * CHUNK)
        x = feats[rows]
        low = (0.5 * x * (1.0 + jnp.tanh(root * (x + cube * x * x * x)))).astype(BF)
        encoded = softplus(dot(win[rows], w_enc))
        mask = 0.5 * jnp.tanh(0.5 * (dot(low, low_mask) + m_bias)) + 0.5
        source = (mask * encoded).astype(BF)
        enc[rows] = encoded
        gate[rows] = mask
        src[rows] = source.astype(F32)
        act[rows] = low.astype(F32)
        dec[rows] = lax.dot_general(
            source, low_dec, (((1,), (1,)), ((), ())), preferred_element_type=F32
        )
    dec[:M] = dec[:M] * edge[:, : 2 * STRIDE]
    for ref in (feats, enc, gate, src, act):
        ref[total:] = jnp.zeros((PADDED * M - total, B), F32)
    for i in range(BLOCKS):
        tgt[i * M : (i + 1) * M] = goal[:, STRIDE * i : STRIDE * (i + 1)]
    estimate = dec[M:total, :STRIDE] + dec[: total - M, STRIDE:]
    count = BLOCKS - 1
    spot = lax.broadcasted_iota(jnp.int32, (count, M, STRIDE), 0)
    late = lax.broadcasted_iota(jnp.int32, (count, M, STRIDE), 2)
    valid = jnp.where(spot * STRIDE + late < lim[:, :STRIDE][None], 1.0, 0.0)
    inside = jnp.where(spot < FRAMES, valid, 0.0).reshape(count * M, STRIDE)
    valid = valid.reshape(count * M, STRIDE)
    error = estimate - tgt[M:total]
    smoothed = jnp.sqrt(error * error + 1.0)
    gest[:M] = jnp.zeros((M, STRIDE), F32)
    gest[M:total] = valid * error / smoothed
    gest[total:] = jnp.zeros((PADDED * M - total, STRIDE), F32)
    loss = jnp.sum(jnp.sum(inside * (smoothed - 1.0), 0, keepdims=True), 1, keepdims=True)
    seen = jnp.sum(jnp.sum(inside, 0, keepdims=True), 1, keepdims=True)
    gm[...] = jnp.zeros_like(gm)
    gm[81:82] = jnp.broadcast_to(loss, (1, B))
    gm[82:83] = jnp.broadcast_to(seen, (1, B))
    for i in range(total // CHUNK):
        at = i * CHUNK + M
        rows = slice(at, at + CHUNK)
        grad_dec = jnp.concatenate(
            [gest[rows], gest[at + M : at + M + CHUNK]], 1
        ).astype(BF)
        mine = own(i * (CHUNK // M), CHUNK // M)
        mine_low = mine.astype(BF)
        gm[64:80] += dot_rows(grad_dec, src[rows].astype(BF) * mine_low)
        grad_source = dot(grad_dec, low_dec)
        mask = gate[rows]
        grad_logit = (grad_source * enc[rows] * mask * (1.0 - mask)).astype(BF)
        enc[rows] = grad_source * mask
        gm[:64] += dot_rows(act[rows].astype(BF), grad_logit * mine_low)
        gm[80:81] += jnp.sum(grad_logit.astype(F32) * mine, 0, keepdims=True)
        x = feats[rows]
        curve = jnp.tanh(root * (x + cube * x * x * x))
        slope = 0.5 * (1.0 + curve) + (0.5 * root) * x * (1.0 - curve * curve) * (
            1.0 + (3.0 * cube) * x * x
        )
        feats[rows] = slope * dot(grad_logit, turned_mask)
    genc[...] = enc[M : M + FRAMES * M]
    for c in range(TILES):
        gres[c, : K * M] = feats[M + c * half : M + c * half + K * M] * live(lim[...], c * HOP, K)
        if nb * RI > K * M:
            gres[c, K * M :] = jnp.zeros((nb * RI - K * M, B), F32)
    send_tiles(gres, send, nb, RI)


def inter_back_kernel(shape, RI, index, grad_rows, rows, h_ref, c_ref, proj, gi, gr, bias, others, send, out, *scratch):
    xs, core = scratch[0], scratch[1:]

    def widen(t, _):
        xs[0, pl.ds(pl.multiple_of(t * RI, 8), RI), :] = rows[t].astype(F32)
        return 0

    lax.fori_loop(0, shape.steps, widen, 0)

    def grads(g, i, r0):
        return jnp.concatenate(
            [grad_rows[i * shape.chunk + j].astype(F32) for j in range(shape.chunk)], 0
        )

    wout = proj_rows(proj, index * 2 * H, 2 * H)
    last = branch_back(shape, grads, xs, h_ref, c_ref, (gi, gr), bias, others, wout, out, core)

    def use(g, i, r0, total):
        for j in range(shape.chunk):
            send[i * shape.chunk + j] = total[j * RI : (j + 1) * RI].astype(BF)

    last(use)


def intra_back(shape, nb, RI, index, gres, lim, x_ref, h_ref, c_ref, proj, gi, gr, bias, others, out, core):
    n = shape.crows

    def grads(g, i, r0):
        return gres[g, pl.ds(r0, n), :]

    wout = proj_rows(proj, index * 2 * H, 2 * H)
    last = branch_back(shape, grads, x_ref, h_ref, c_ref, (gi, gr), bias, others, wout, out, core)

    def use(g, i, r0, total):
        gres[g, pl.ds(r0, n), :] = gres[g, pl.ds(r0, n), :] + total

    last(use)


def third_back_kernel(shape, nb, RI, index, gres_in, back, lim, x_ref, h_ref, c_ref, proj, gi, gr, bias, others, gres, send, out, *core):
    gres[...] = gres_in[...]
    add_tiles(gres, back, nb, RI, lim[...], None)
    intra_back(shape, nb, RI, index, gres, lim, x_ref, h_ref, c_ref, proj, gi, gr, bias, others, out, core)
    for c in range(TILES):
        gres[c, : K * M] = gres[c, : K * M] * live(lim[...], c * HOP, K)
    send_tiles(gres, send, nb, RI)


def first_back_kernel(shape, nb, RI, gres_in, back, lim, x_ref, h_ref, c_ref, proj, gi, gr, bias, others, vec, win, genc, out, gm, gres, bottle, *core):
    gres[...] = gres_in[...]
    add_tiles(gres, back, nb, RI, lim[...], None)
    intra_back(shape, nb, RI, 0, gres, lim, x_ref, h_ref, c_ref, proj, gi, gr, bias, others, out, core)
    half = HOP * M
    bottle[...] = jnp.zeros_like(bottle)
    for c in range(TILES):
        at = (c * HOP + 1) * M
        bottle[at : at + K * M] += gres[c, : K * M]
    w_enc = proj_rows(proj, BASE + N + B, 2 * STRIDE).astype(BF)
    turned_bn = jnp.transpose(proj_rows(proj, BASE, N)).astype(BF)
    gain, beta = vec[0:1], vec[1:2]
    gm[...] = jnp.zeros_like(gm)
    own_rows = FRAMES * M
    for i in range(BLOCKS * M // CHUNK):
        at = i * CHUNK
        rows = slice(at, at + CHUNK)
        pre = dot(win[rows], w_enc)
        unit, scale = norm_parts(softplus(pre))
        normed = (unit * gain + beta).astype(BF)
        low = (bottle[rows] * live(lim[...], i * (CHUNK // M) - 1, CHUNK // M)).astype(BF)
        gm[:64] += dot_rows(normed, low)
        gm[80:81] += jnp.sum(low.astype(F32), 0, keepdims=True)
        grad_normed = dot(low, turned_bn)
        gm[81:82] += jnp.sum(grad_normed * unit, 0, keepdims=True)
        gm[82:83] += jnp.sum(grad_normed, 0, keepdims=True)
        grad_enc = norm_back(grad_normed, unit, scale, gain)
        lo, hi = max(at - M, 0), min(at + CHUNK - M, own_rows)
        if lo < hi:
            piece = genc[lo:hi]
            above, below = lo + M - at, at + CHUNK - M - hi
            if above:
                piece = jnp.concatenate([jnp.zeros((above, B), F32), piece], 0)
            if below:
                piece = jnp.concatenate([piece, jnp.zeros((below, B), F32)], 0)
            grad_enc = grad_enc + piece
        grad_pre = (grad_enc * (0.5 * jnp.tanh(0.5 * pre) + 0.5)).astype(BF)
        gm[64:80] += dot_rows(win[rows], grad_pre)


def call(kernel, outs, ins, scratch, index=None):
    if index is None:
        specs = [pl.BlockSpec(memory_space=pltpu.VMEM)] * len(ins)
        extra = []
        wrapped = kernel
    else:
        big = [i for i, a in enumerate(ins) if a.ndim == 4 and a.shape[:2] == (2 * LAYERS, 2)]
        small = [i for i, a in enumerate(ins) if a.ndim == 3 and a.shape[0] == 2 * LAYERS]
        specs = [
            pl.BlockSpec(memory_space=pl.ANY if i in big else pltpu.VMEM) for i in range(len(ins))
        ]
        extra = [pltpu.VMEM((1,) + ins[i].shape[1:], F32) for i in big]
        extra.append(pltpu.SemaphoreType.DMA((len(big),)))

        def wrapped(*refs):
            refs = list(refs)
            held, sem = refs[len(refs) - len(extra) : -1], refs[-1]
            copies = []
            for j, i in enumerate(big):
                copies.append(pltpu.make_async_copy(refs[i].at[pl.ds(index, 1)], held[j], sem.at[j]))
                copies[-1].start()
            for copy in copies:
                copy.wait()
            for j, i in enumerate(big):
                refs[i] = held[j]
            for i in small:
                refs[i] = refs[i].at[pl.ds(index, 1)]
            kernel(*refs[: len(refs) - len(extra)])

    return pl.pallas_call(
        wrapped,
        out_shape=outs,
        in_specs=specs,
        out_specs=[pl.BlockSpec(memory_space=pltpu.VMEM)] * len(outs),
        scratch_shapes=list(scratch) + extra,
        compiler_params=pltpu.CompilerParams(vmem_limit_bytes=56 * 1024 * 1024),
    )(*ins)


def shift(block, axis, distance):
    size = lax.axis_size(axis)
    route = [(i, i + distance) for i in range(size) if 0 <= i + distance < size]
    return lax.ppermute(block, axis, route)


def exchange(block):
    return lax.all_to_all(block, "block", split_axis=0, concat_axis=0, tiled=True)


def adam_step(grad, moment, square, weight, average, decay):
    moment = BETA_ONE * moment + (1.0 - BETA_ONE) * grad
    square = BETA_TWO * square + (1.0 - BETA_TWO) * grad * grad
    corrected = moment / (1.0 - BETA_ONE**STEP)
    scaled = square / (1.0 - BETA_TWO**STEP)
    weight = weight - RATE * (corrected / (jnp.sqrt(scaled) + ADAM_EPS) + decay * weight)
    average = KEEP * average + (1.0 - KEEP) * weight
    return (moment, square, weight, average)


def body(
    mixture,
    target,
    lengths,
    input_gates,
    recur_gates,
    projections,
    vectors,
    moment_input,
    moment_recur,
    moment_proj,
    moment_vecs,
    square_input,
    square_recur,
    square_proj,
    square_vecs,
    average_input,
    average_recur,
    average_proj,
    average_vecs,
):
    nb = lax.axis_size("block")
    place = lax.axis_index("block")
    RI = -(-K // nb) * M
    intra = Shape(TILES, K, M)
    inter = Shape(1, TILES * nb, RI)
    T = inter.steps
    gi, gr, proj = input_gates, recur_gates, projections
    lim = jnp.broadcast_to((lengths - place * (FRAMES * STRIDE))[:, None], (M, B))
    edge = jnp.broadcast_to((place > 0).astype(F32), (M, B))
    periods = vectors[2 * N + B : 2 * N + B + 2 * LAYERS * PERIOD].reshape(2 * LAYERS, PERIOD)
    bias = periods[:, : 8 * H].reshape(2 * LAYERS, 2, 4 * H)
    others = periods[:, 8 * H :].reshape(2 * LAYERS, 3, B)
    vec = jnp.concatenate([vectors[: 2 * N + B], vectors[-N:]]).reshape(4, N)
    waves = jnp.stack([mixture, target])
    reach = (HOP + 2) * STRIDE
    following = shift(waves[:, :, :reach], "block", -1)
    leading = shift(mixture[:, -STRIDE:], "block", 1)
    rest = jnp.zeros((2, M, 14 * 128 - STRIDE - FRAMES * STRIDE - reach), F32)
    leading = jnp.stack([leading, jnp.zeros_like(leading)])
    waves = jnp.concatenate([leading, waves, following, rest], 2)

    res_shape = SDS((TILES, nb * RI, B), F32)
    send_shape = SDS((nb, TILES, RI, B), BF)
    x_shape = SDS((TILES, K * M, B), BF)

    def state(shape):
        return SDS((shape.groups, shape.wide, 2 * H), F32)

    def fwd_scratch(shape):
        return [
            pltpu.VMEM((2, B, 4 * H), BF),
            pltpu.VMEM((2, H, 4 * H), BF),
            pltpu.VMEM((2, shape.groups, shape.size, 4 * H), F32),
        ]

    res0, send, x0, h0, c0, win = call(
        functools.partial(first_kernel, intra, nb, RI),
        [res_shape, send_shape, x_shape, state(intra), state(intra), SDS((BLOCKS * M, 2 * STRIDE), BF)],
        [waves[0], lim, proj, vec, gi, gr, bias, others],
        fwd_scratch(intra)
        + [pltpu.VMEM((BLOCKS * M, 2 * STRIDE), F32), pltpu.VMEM((BLOCKS * M, B), F32)],
        0,
    )

    def inter_step(send, index):
        rows = exchange(send).reshape(T, RI, B)
        normed, h, c = call(
            functools.partial(inter_kernel, inter, RI, index),
            [SDS((T, RI, B), BF), state(inter), state(inter)],
            [rows, proj, gi, gr, bias, others],
            fwd_scratch(inter) + [pltpu.VMEM((1, inter.size, B), F32)],
            index,
        )
        return rows, h, c, exchange(normed.reshape(nb, TILES, RI, B))

    rows1, h1, c1, back = inter_step(send, 1)
    res2, send, x2, h2, c2 = call(
        functools.partial(third_kernel, intra, nb, RI, 2),
        [res_shape, send_shape, x_shape, state(intra), state(intra)],
        [res0, back, lim, proj, gi, gr, bias, others],
        fwd_scratch(intra),
        2,
    )
    rows3, h3, c3, back = inter_step(send, 3)
    edge_shape = SDS(((HOP + 1) * M, B), F32)
    part, up, down = call(
        functools.partial(part_kernel, nb, RI),
        [SDS(((FRAMES + HOP) * M, B), F32), edge_shape, edge_shape],
        [res2, back, lim],
        [pltpu.VMEM(res_shape.shape, F32)],
    )
    before = shift(up, "block", 1)
    after = shift(down, "block", -1)
    tall = PADDED * M
    send, gres, genc, gm_mid = call(
        functools.partial(middle_kernel, nb, RI),
        [send_shape, res_shape, SDS((FRAMES * M, B), F32), SDS((88, B), F32)],
        [part, before, after, lim, edge, win, waves[1], proj, vec],
        [
            pltpu.VMEM((tall, B), F32),
            pltpu.VMEM((tall, 2 * STRIDE), F32),
            pltpu.VMEM((tall, STRIDE), F32),
            pltpu.VMEM((tall, STRIDE), F32),
            pltpu.VMEM((tall, B), F32),
            pltpu.VMEM((tall, B), F32),
            pltpu.VMEM((tall, B), F32),
            pltpu.VMEM((tall, B), F32),
        ],
    )
    out_shape = SDS((ROWS_G, 4 * H), F32)

    def inter_back(send, rows, h, c, index):
        grad_rows = exchange(send).reshape(T, RI, B)
        send, out = call(
            functools.partial(inter_back_kernel, inter, RI, index),
            [SDS((T, RI, B), BF), out_shape],
            [grad_rows, rows, h, c, proj, gi, gr, bias, others],
            [pltpu.VMEM((1, inter.size, B), F32)] + back_scratch(inter),
            index,
        )
        return exchange(send.reshape(nb, TILES, RI, B)), out

    back, out3 = inter_back(send, rows3, h3, c3, 3)
    gres, send, out2 = call(
        functools.partial(third_back_kernel, intra, nb, RI, 2),
        [res_shape, send_shape, out_shape],
        [gres, back, lim, x2, h2, c2, proj, gi, gr, bias, others],
        back_scratch(intra),
        2,
    )
    back, out1 = inter_back(send, rows1, h1, c1, 1)
    out0, gm_first = call(
        functools.partial(first_back_kernel, intra, nb, RI),
        [out_shape, SDS((88, B), F32)],
        [gres, back, lim, x0, h0, c0, proj, gi, gr, bias, others, vec, win, genc],
        [pltpu.VMEM(res_shape.shape, F32), pltpu.VMEM((BLOCKS * M, B), F32)] + back_scratch(intra),
        0,
    )
    outs = jnp.stack([out0, out1, out2, out3])
    outs, gm_mid, gm_first = lax.psum((outs, gm_mid, gm_first), ("block", "dp"))
    total_loss, total_count = gm_mid[81, 0], gm_mid[82, 0]
    grad_input = outs[:, :128].reshape(2 * LAYERS, 2, B, 4 * H)
    grad_recur = outs[:, 128:384].reshape(2 * LAYERS, 2, H, 4 * H)
    turned = outs[:, 384:416].reshape(2 * LAYERS, 32, 2, 2 * H)
    turned = jnp.transpose(turned, (0, 3, 2, 1)).reshape(4 * LAYERS * H, B)
    grad_proj = jnp.concatenate(
        [turned, gm_first[:64], gm_mid[:64], gm_first[64:80], gm_mid[64:80]], 0
    )
    rows = jnp.concatenate(
        [outs[:, 416:418].reshape(2 * LAYERS, 8 * H), outs[:, 418:421, :B].reshape(2 * LAYERS, 3 * B)], 1
    )
    grad_vecs = jnp.concatenate(
        [gm_first[81], gm_first[82], gm_first[80], rows.reshape(-1), gm_mid[80]]
    )
    grads = (grad_input, grad_recur, grad_proj, grad_vecs)
    params = (input_gates, recur_gates, projections, vectors)
    moments = (moment_input, moment_recur, moment_proj, moment_vecs)
    seconds = (square_input, square_recur, square_proj, square_vecs)
    averages = (average_input, average_recur, average_proj, average_vecs)
    squared = sum((jnp.sum(g * g) for g in grads))
    grad_norm = jnp.sqrt(squared) / total_count
    factor = jnp.minimum(1.0, CLIP / grad_norm) / total_count
    decays = (DECAY, DECAY, DECAY, 0.0)
    results = [
        adam_step(grads[i] * factor, moments[i], seconds[i], params[i], averages[i], decays[i])
        for i in range(4)
    ]
    kinds = [[r[j] for r in results] for j in range(4)]
    copies = [m.astype(BF) for m in kinds[2]]
    return (total_loss, total_count, grad_norm, *kinds[0], *kinds[1], *kinds[2], *kinds[3], *copies)


def solution(mesh):
    in_specs = (P("dp", "block"), P("dp", "block"), P("dp")) + (P(),) * 16
    return jax.shard_map(
        body, mesh=mesh, in_specs=in_specs, out_specs=(P(),) * 23, check_vma=False
    )
```

profile of v0, /device:TPU:0, one launch (start us, length us, event | category | flops | bytes accessed | tf_op | source)
XLA Modules:
  0.0 564.4 jit_solution(14866402605463515494)
XLA Ops:
  8.0 4.9 collective-permute-start
  20.8 2.1 copy.70.refs_2_.refs_1_.refs_3_.proj.refs_4_.refs_6_
  24.3 26.6 %shard_map.362 = (f32[3,832,64]{2,1,0:T(8,128)}, bf16[8,3,104,64]{3,2,1,0:T(8,128)(2,1)}, bf16[3,800,64]{2,1,0:T(8,128)(2,1)}, f32[3,816,256]{2,1,0:T(8,128)}, f...) custom-call(f32[8,1792]{1,0:T(8,128)} %get-tuple-element.108.refs_0_, s32[8,64]{1,0:T(8,128)} %broadcast_in_dim.13.refs_1_.refs_2_.lim, ...), custom_call_target="tpu_custom_call" | custom-call | tf_op jit(solution)/shard_map/pallas_call | solution.py:600
  52.3 18.3 %all_to_all.40 = bf16[8,3,104,64]{2,3,1,0:T(8,128)(2,1)S(1)} all-to-all(bf16[8,3,104,64]{2,3,1,0:T(8,128)(2,1)S(1)} %copy.71), channel_id=1, replica_groups=mesh['block'=8,'dp'=4] {'block'}, dimensions={0} | all-to-all | bytes 638976 | tf_op jit(solution)/shard_map/all_to_all | solution.py:617
  71.6 13.6 %shard_map.363 = (bf16[24,104,64]{2,1,0:T(8,128)(2,1)}, f32[1,2704,256]{2,1,0:T(8,128)}, f32[1,2704,256]{2,1,0:T(8,128)}) custom-call(bf16[24,104,64]{2,1,0:T(8,128)(2,1)} %bitcast.41, f32[1184,64]{1,0:T(8,128)} %copy.70.refs_2_.refs_1_.refs_3_.proj.refs_4_.refs_6_, f32[4,2,64,512]{3,2,1,0:T(8,128)} %refs_7_.3, f32[4,2,128,512]{3,2,1,0:T(8,128)} %refs_8_.3, ...), custom_call_target="tpu_custom_call" | custom-call | tf_op jit(solution)/shard_map/pallas_call | solution.py:600
  86.6 14.6 %all_to_all.41 = bf16[8,3,104,64]{2,3,1,0:T(8,128)(2,1)S(1)} all-to-all(bf16[8,3,104,64]{2,3,1,0:T(8,128)(2,1)S(1)} %copy.74), channel_id=1, replica_groups=mesh['block'=8,'dp'=4] {'block'}, dimensions={0} | all-to-all | bytes 638976 | tf_op jit(solution)/shard_map/all_to_all | solution.py:617
  102.3 25.9 %shard_map.364 = (f32[3,832,64]{2,1,0:T(8,128)}, bf16[8,3,104,64]{3,2,1,0:T(8,128)(2,1)}, bf16[3,800,64]{2,1,0:T(8,128)(2,1)}, f32[3,816,256]{2,1,0:T(8,128)}, f32[3,816,256]{2,1,0:T(8,128)}) custom-call(f32[3,832,64]{2,1,0:T(8,128)} %get-tuple-element.56.refs_0_, bf16[8,3,104,64]{3,2,1,0:T(8,128)(2,1)} %copy.75.refs_1_, ...), custom_call_target="tpu_custom_call" | custom-call | tf_op jit(solution)/shard_map/pallas_call | solution.py:600
  129.6 14.6 %all_to_all.42 = bf16[8,3,104,64]{2,3,1,0:T(8,128)(2,1)S(1)} all-to-all(bf16[8,3,104,64]{2,3,1,0:T(8,128)(2,1)S(1)} %copy.77), channel_id=1, replica_groups=mesh['block'=8,'dp'=4] {'block'}, dimensions={0} | all-to-all | bytes 638976 | tf_op jit(solution)/shard_map/all_to_all | solution.py:617
  145.3 13.6 %shard_map.365 = (bf16[24,104,64]{2,1,0:T(8,128)(2,1)}, f32[1,2704,256]{2,1,0:T(8,128)}, f32[1,2704,256]{2,1,0:T(8,128)}) custom-call(bf16[24,104,64]{2,1,0:T(8,128)(2,1)} %bitcast.43, f32[1184,64]{1,0:T(8,128)} %copy.70.refs_2_.refs_1_.refs_3_.proj.refs_4_.refs_6_, f32[4,2,64,512]{3,2,1,0:T(8,128)} %refs_7_.3, f32[4,2,128,512]{3,2,1,0:T(8,128)} %refs_8_.3, ...), custom_call_target="tpu_custom_call" | custom-call | tf_op jit(solution)/shard_map/pallas_call | solution.py:600
  160.3 14.6 %all_to_all.43 = bf16[8,3,104,64]{2,3,1,0:T(8,128)(2,1)S(1)} all-to-all(bf16[8,3,104,64]{2,3,1,0:T(8,128)(2,1)S(1)} %copy.80), channel_id=1, replica_groups=mesh['block'=8,'dp'=4] {'block'}, dimensions={0} | all-to-all | bytes 638976 | tf_op jit(solution)/shard_map/all_to_all | solution.py:617
  176.0 2.8 shard_map.366
  178.8 3.0 collective-permute-start.2
  181.8 1.8 collective-permute-start.3
  183.6 6.3 %collective-permute-done.2.before = f32[408,64]{1,0:T(8,128)S(1)} collective-permute-done((f32[408,64]{1,0:T(8,128)}, f32[408,64]{1,0:T(8,128)S(1)}, u32[]{:S(2)}, u32[]{:S(2)}) %collective-permute-start.2) | collective-permute-done | bytes 104480 | tf_op jit(solution)/shard_map/ppermute | solution.py:613
  190.6 6.4 %shard_map.367 = (bf16[8,3,104,64]{3,2,1,0:T(8,128)(2,1)}, f32[3,832,64]{2,1,0:T(8,128)}, f32[1200,64]{1,0:T(8,128)}, f32[88,64]{1,0:T(8,128)}) custom-call(f32[1600,64]{1,0:T(8,128)} %get-tuple-element.62.part, f32[408,64]{1,0:T(8,128)} %copy-done.16, f32[408,64]{1,0:T(8,128)} %copy-done.17, s32[8,64]{1,0:T(8,128)} %broadcast_in_dim.13.refs_1_.refs_2_.lim, ...), custom_call_target="tpu_custom_call" | custom-call | tf_op jit(solution)/shard_map/pallas_call | solution.py:600
  198.4 16.8 %all_to_all.44 = bf16[8,3,104,64]{2,3,1,0:T(8,128)(2,1)S(1)} all-to-all(bf16[8,3,104,64]{2,3,1,0:T(8,128)(2,1)S(1)} %copy.83), channel_id=1, replica_groups=mesh['block'=8,'dp'=4] {'block'}, dimensions={0} | all-to-all | bytes 638976 | tf_op jit(solution)/shard_map/all_to_all | solution.py:617
  216.3 21.9 %shard_map.368 = (bf16[24,104,64]{2,1,0:T(8,128)(2,1)}, f32[424,512]{1,0:T(8,128)}) custom-call(bf16[24,104,64]{2,1,0:T(8,128)(2,1)} %bitcast.46, bf16[24,104,64]{2,1,0:T(8,128)(2,1)} %bitcast.44, f32[1,2704,256]{2,1,0:T(8,128)} %get-tuple-element.69.refs_2_, f32[1,2704,256]{2,1,0:T(8,128)} %get-tuple-element.70.refs_3_, ...), custom_call_target="tpu_custom_call" | custom-call | tf_op jit(solution)/shard_map/pallas_call | solution.py:600
  239.5 15.2 %all_to_all.45 = bf16[8,3,104,64]{2,3,1,0:T(8,128)(2,1)S(1)} all-to-all(bf16[8,3,104,64]{2,3,1,0:T(8,128)(2,1)S(1)} %copy.86), channel_id=1, replica_groups=mesh['block'=8,'dp'=4] {'block'}, dimensions={0} | all-to-all | bytes 638976 | tf_op jit(solution)/shard_map/all_to_all | solution.py:617
  255.8 31.9 %shard_map.369 = (f32[3,832,64]{2,1,0:T(8,128)}, bf16[8,3,104,64]{3,2,1,0:T(8,128)(2,1)}, f32[424,512]{1,0:T(8,128)}) custom-call(f32[3,832,64]{2,1,0:T(8,128)} %get-tuple-element.67.refs_0_, bf16[8,3,104,64]{3,2,1,0:T(8,128)(2,1)} %copy.87.refs_1_, s32[8,64]{1,0:T(8,128)} %broadcast_in_dim.13.refs_1_.refs_2_.lim, ...), custom_call_target="tpu_custom_call" | custom-call | tf_op jit(solution)/shard_map/pallas_call | solution.py:600
  289.0 14.8 %all_to_all.46 = bf16[8,3,104,64]{2,3,1,0:T(8,128)(2,1)S(1)} all-to-all(bf16[8,3,104,64]{2,3,1,0:T(8,128)(2,1)S(1)} %copy.89), channel_id=1, replica_groups=mesh['block'=8,'dp'=4] {'block'}, dimensions={0} | all-to-all | bytes 638976 | tf_op jit(solution)/shard_map/all_to_all | solution.py:617
  304.9 21.9 %shard_map.370 = (bf16[24,104,64]{2,1,0:T(8,128)(2,1)}, f32[424,512]{1,0:T(8,128)}) custom-call(bf16[24,104,64]{2,1,0:T(8,128)(2,1)} %bitcast.47, bf16[24,104,64]{2,1,0:T(8,128)(2,1)} %bitcast.42, f32[1,2704,256]{2,1,0:T(8,128)} %get-tuple-element.77.refs_2_, f32[1,2704,256]{2,1,0:T(8,128)} %get-tuple-element.78.refs_3_, ...), custom_call_target="tpu_custom_call" | custom-call | tf_op jit(solution)/shard_map/pallas_call | solution.py:600
  328.2 14.9 %all_to_all.47 = bf16[8,3,104,64]{2,3,1,0:T(8,128)(2,1)S(1)} all-to-all(bf16[8,3,104,64]{2,3,1,0:T(8,128)(2,1)S(1)} %copy.92), channel_id=1, replica_groups=mesh['block'=8,'dp'=4] {'block'}, dimensions={0} | all-to-all | bytes 638976 | tf_op jit(solution)/shard_map/all_to_all | solution.py:617
  344.1 34.3 %shard_map.371 = (f32[424,512]{1,0:T(8,128)}, f32[88,64]{1,0:T(8,128)}) custom-call(f32[3,832,64]{2,1,0:T(8,128)} %get-tuple-element.75.refs_0_, bf16[8,3,104,64]{3,2,1,0:T(8,128)(2,1)} %copy.93.refs_1_, s32[8,64]{1,0:T(8,128)} %broadcast_in_dim.13.refs_1_.refs_2_.lim, bf16[3,800,64]{2,1,0:T(8,128)(2,1)} %get-tuple-element.80.refs_3_, ...), custom_call_target="tpu_custom_call" | custom-call | tf_op jit(solution)/shard_map/pallas_call | solution.py:600
  378.5 3.3 pad_maximum_fusion
  382.6 40.5 %all-reduce.1 = (f32[88,64]{1,0:T(8,128)S(1)}, f32[88,64]{1,0:T(8,128)S(1)}) all-reduce(f32[88,64]{1,0:T(8,128)S(1)} %copy-done.20, f32[88,64]{1,0:T(8,128)S(1)} %copy-done.21), channel_id=1, replica_groups=mesh['block'=8,'dp'=4] {'block','dp'}, use_global_device_ids=true, to_apply=%region_0.0 | all-reduce | flops 11264 | bytes 90112 | tf_op jit(solution)/shard_map/psum | solution.py:770
  426.4 93.5 %all-reduce.4.cloned.1.call-done = f32[4,424,512]{2,1,0:T(8,128)} async-done(((f32[4,424,512]{2,1,0:T(8,128)}), f32[4,424,512]{2,1,0:T(8,128)}) %all-reduce.4.cloned.1.call-update) | async-done | bytes 3473424 | tf_op jit(solution)/shard_map/psum | solution.py:770
  526.3 1.8 concatenate.17
  529.8 2.7 multiply_reduce_fusion
  540.2 2.4 fusion.7
  544.4 2.1 fusion.11
  550.2 3.7 fusion.9
  553.9 2.0 multiply_add_fusion
  (116 shorter events, 50.8 us)
Async XLA Ops:
  7.2 512.8 %all-reduce.4.cloned.1.call-start = ((), (), s32[]{:S(2)}) async-start(), calls=%async_computation.8 | async-start | bytes 6946816 | tf_op jit(solution)/shard_map/psum | solution.py:770
  8.0 14.8 %collective-permute-start = (f32[8,8]{1,0:T(8,128)S(1)}, f32[8,8]{1,0:T(8,128)S(1)}, u32[]{:S(2)}, u32[]{:S(2)}) collective-permute-start(f32[8,8]{1,0:T(8,128)S(1)} %slice.72), channel_id=1, source_target_pairs={{0,4},{4,8},{8,12},{12,16},{16,20},{20,24},{24,28},{1,5},{5,9},{9,... | collective-permute-start | bytes 776 | tf_op jit(solution)/shard_map/ppermute | solution.py:613
  13.6 9.2 %collective-permute-start.1 = (f32[2,8,416]{2,1,0:T(8,128)S(1)}, f32[2,8,416]{2,1,0:T(8,128)S(1)}, u32[]{:S(2)}, u32[]{:S(2)}) collective-permute-start(f32[2,8,416]{2,1,0:T(8,128)S(1)} %fusion.3), channel_id=1, source_target_pairs={{4,0},{8,4},{12,8},{16,12},{20,16},{24,20},{28,24},{5,1},{9,5},{13... | collective-permute-start | bytes 79880 | tf_op jit(solution)/shard_map/ppermute | solution.py:613
  178.8 11.1 %collective-permute-start.2 = (f32[408,64]{1,0:T(8,128)}, f32[408,64]{1,0:T(8,128)S(1)}, u32[]{:S(2)}, u32[]{:S(2)}) collective-permute-start(f32[408,64]{1,0:T(8,128)} %get-tuple-element.63), channel_id=1, source_target_pairs={{0,4},{4,8},{8,12},{12,16},{16,20},{20,24},{24,28},{1,5},{5,9},{9,... | collective-permute-start | bytes 313352 | tf_op jit(solution)/shard_map/ppermute | solution.py:613
  181.8 8.1 %collective-permute-start.3 = (f32[408,64]{1,0:T(8,128)}, f32[408,64]{1,0:T(8,128)S(1)}, u32[]{:S(2)}, u32[]{:S(2)}) collective-permute-start(f32[408,64]{1,0:T(8,128)} %get-tuple-element.64), channel_id=1, source_target_pairs={{4,0},{8,4},{12,8},{16,12},{20,16},{24,20},{28,24},{5,1},{9,5},{13... | collective-permute-start | bytes 313352 | tf_op jit(solution)/shard_map/ppermute | solution.py:613
  189.9 0.7 copy-start.16
  189.9 0.7 copy-start.17
  344.1 34.3 %copy-start.12 = (f32[424,512]{1,0:T(8,128)S(1)}, f32[424,512]{1,0:T(8,128)}, u32[]{:S(2)}) copy-start(f32[424,512]{1,0:T(8,128)} %get-tuple-element.87) | copy-start | bytes 2605060
  344.1 34.3 %copy-start.13 = (f32[424,512]{1,0:T(8,128)S(1)}, f32[424,512]{1,0:T(8,128)}, u32[]{:S(2)}) copy-start(f32[424,512]{1,0:T(8,128)} %get-tuple-element.86) | copy-start | bytes 2605060
  344.1 34.3 %copy-start.14 = (f32[424,512]{1,0:T(8,128)S(1)}, f32[424,512]{1,0:T(8,128)}, u32[]{:S(2)}) copy-start(f32[424,512]{1,0:T(8,128)} %get-tuple-element.85) | copy-start | bytes 2605060
  381.7 0.8 copy-start.20
  381.8 0.8 copy-start.21
  524.3 8.2 %copy-start.2 = (f32[4,424,512]{2,1,0:T(8,128)S(1)}, f32[4,424,512]{2,1,0:T(8,128)}, u32[]{:S(2)}) copy-start(f32[4,424,512]{2,1,0:T(8,128)} %all-reduce.4.cloned.1.call-done) | copy-start | bytes 10420228
  526.3 11.1 %copy-start.18 = (f32[5120]{0:T(1024)S(1)}, f32[5120]{0:T(1024)}, u32[]{:S(2)}) copy-start(f32[5120]{0:T(1024)} %param.25) | copy-start | bytes 61444
  537.4 5.2 copy-start.15
  538.9 4.7 copy-start.19
  540.2 3.3 copy-start.10
  542.6 3.9 copy-start.8
  542.6 1.5 copy-start.1
  542.6 1.8 copy-start.9
  544.4 2.1 copy-start.11
  546.5 1.6 copy-start.4
  546.5 2.3 copy-start.6
  547.7 1.9 copy-start
  547.7 2.5 copy-start.5
  550.2 3.7 copy-start.7
  553.9 2.0 copy-start.3
Sparse Core Ops, SparseCore 0:
  381.9 138.0 all-reduce.3
where the time goes:
time: 574 us; the launch traced here: 564 us
  Pallas kernels  199 us (35%)
  blocking collectives  164 us (29%)
  waiting for transfers between devices  99.9 us (17%)
  local copies, waits for them, and re-layouts  42.7 us (7%)
  other arithmetic  26.8 us (5%)
  between operations  20.7 us (4%)
  starting transfers between devices  11 us (2%)
    pallas_call x10, Pallas kernels, call(): pl.pallas_call(wrapped, out_shape=outs, in_specs=specs, out_specs=[pl.Blo...  199 us
    all_to_all x8, blocking collectives, exchange(): lax.all_to_all(block, 'block', split_axis=0, concat_axis=0, tiled=True)  124 us
    psum x1, waiting for transfers between devices, body(): outs, gm_mid, gm_first = lax.psum((outs, gm_mid, gm_first), ('block', 'dp'))  93.5 us
    psum x1, blocking collectives, body(): outs, gm_mid, gm_first = lax.psum((outs, gm_mid, gm_first), ('block', 'dp'))  40.5 us
  transfers between devices with their start and end apart: 5, of which 2 were waited for; matrix products, arithmetic and copies ran while one was open for 2% of the time, Pallas kernels for 0%

commit v1 on v0

v1 whole, which is shorter than its diff:
```python
import functools

import jax
import jax.numpy as jnp
from jax import lax
from jax.experimental import pallas as pl
from jax.experimental.pallas import tpu as pltpu
from jax.sharding import PartitionSpec as P

N = 64
B = 64
H = 128
K = 100
STRIDE = 8
LAYERS = 2
STEP = 10
HOP = 50
TILES = 3
M = 8
FRAMES = 150
BASE = 4 * LAYERS * H
PERIOD = 8 * H + 3 * B
ROWS_MAPS = 1536
ROWS_VECS = 1664
ROWS_G = 1696
ROWS_FIRST = 1856
LANES = 128
BLOCKS = 208
PADDED = 216
CHUNK = 416

EPS_NORM = 1e-05
CLIP = 0.001
RATE = 0.1
BETA_ONE = 0.9
BETA_TWO = 0.999
ADAM_EPS = 1e-08
DECAY = 0.01
KEEP = 0.9

BF = jnp.bfloat16
F32 = jnp.float32
SDS = jax.ShapeDtypeStruct


def dot(left, right):
    return jnp.dot(left, right, preferred_element_type=F32)


def dot_turned(left, right):
    return lax.dot_general(left, right, (((1,), (1,)), ((), ())), preferred_element_type=F32)


def dot_rows(left, right):
    return lax.dot_general(left, right, (((0,), (0,)), ((), ())), preferred_element_type=F32)


def half_scale():
    lane = lax.broadcasted_iota(jnp.int32, (1, 4 * H), 1)
    return jnp.where((lane >= 2 * H) & (lane < 3 * H), 1.0, 0.5)


def gate_acts(z):
    act = jnp.tanh(z)
    sig_i = 0.5 * act[:, :H] + 0.5
    sig_f = 0.5 * act[:, H : 2 * H] + 0.5
    sig_o = 0.5 * act[:, 3 * H :] + 0.5
    return sig_i, sig_f, act[:, 2 * H : 3 * H], sig_o


def norm_parts(value):
    center = value - jnp.mean(value, -1, keepdims=True)
    spread = jnp.mean(center * center, -1, keepdims=True)
    scale = lax.rsqrt(spread + EPS_NORM)
    return center * scale, scale


def norm_back(grad, unit, scale, gain):
    inner = grad * gain
    return scale * (
        inner
        - jnp.mean(inner, -1, keepdims=True)
        - unit * jnp.mean(inner * unit, -1, keepdims=True)
    )


def live(lim, start, count):
    pos = lax.broadcasted_iota(jnp.int32, (count, M, B), 0) + start
    return jnp.where(pos * STRIDE < lim[None], 1.0, 0.0).reshape(count * M, B)


def limits(lengths):
    row = lax.broadcasted_iota(jnp.int32, (M, B), 0)
    total = jnp.zeros((M, B), jnp.int32)
    for m in range(M):
        total = jnp.where(row == m, lengths[m], total)
    return total - lax.axis_index("block") * (FRAMES * STRIDE)


def pieces(vectors, start, count):
    parts = []
    at = start
    while at < start + count:
        wide = at % 2 == 0 and at + 2 <= start + count
        lane = (at % 2) * N
        parts.append(vectors[at // 2 : at // 2 + 1, lane : lane + (2 * N if wide else N)])
        at += 2 if wide else 1
    return parts[0] if len(parts) == 1 else jnp.concatenate(parts, 1)


def branch_vectors(vectors, index):
    first = (2 * N + B + index * PERIOD) // N
    half = half_scale()
    bias = [pieces(vectors, first + 8 * d, 8) * half for d in range(2)]
    return bias, [pieces(vectors, first + 16 + j, 1) for j in range(3)]


def own(start, count):
    pos = lax.broadcasted_iota(jnp.int32, (count, M, B), 0) + start
    return jnp.where(pos < FRAMES, 1.0, 0.0).reshape(count * M, B)


def chunk_of(steps, rows):
    best = 1
    for size in range(1, steps + 1):
        if steps % size == 0 and size * rows <= 512 and size * rows % 16 == 0:
            best = size
    return best


class Shape:
    def __init__(self, groups, steps, rows):
        self.groups, self.steps, self.rows = groups, steps, rows
        self.size = steps * rows
        self.chunk = chunk_of(steps, rows)
        self.crows = self.chunk * rows
        self.chunks = steps // self.chunk
        self.wide = (steps + 2) * rows
        self.unroll = 4 if steps % 4 == 0 else 1


def chunk_loop(shape, fn):
    for g in range(shape.groups):

        def step(i, _, g=g):
            fn(g, i, pl.multiple_of(i * shape.crows, 8))
            return 0

        lax.fori_loop(0, shape.chunks, step, 0)


def forward_weights(gi, gr, wi, wr):
    half = half_scale()
    for d in range(2):
        wi[d] = (gi[0, d].astype(BF).astype(F32) * half).astype(BF)
        wr[d] = (gr[0, d].astype(BF).astype(F32) * half).astype(BF)


def lstm_scan(shape, pg, wr, h_ref, c_ref):
    G, S, R = shape.groups, shape.steps, shape.rows
    pad = jnp.zeros((R, 2 * H), F32)
    for g in range(G):
        for ref in (h_ref, c_ref):
            ref[g, :R] = pad
            ref[g, (S + 1) * R :] = pad

    def one(d, t, hidden, memory):
        at = pl.multiple_of(t * R, 8)
        pre = jnp.concatenate([pg[d, g, pl.ds(at, R), :] for g in range(G)], 0)
        z = pre + dot(hidden, wr[d])
        sig_i, sig_f, tan_g, sig_o = gate_acts(z)
        memory = sig_f * memory + sig_i * tan_g
        hidden = (sig_o * jnp.tanh(memory)).astype(BF)
        full = hidden.astype(F32)
        after = pl.multiple_of(t * R + R, 8)
        for g in range(G):
            h_ref[g, pl.ds(after, R), d * H : (d + 1) * H] = full[g * R : (g + 1) * R]
            c_ref[g, pl.ds(after, R), d * H : (d + 1) * H] = memory[g * R : (g + 1) * R]
        return hidden, memory

    def step(s, carry):
        hf, cf, hb, cb = carry
        hf, cf = one(0, s, hf, cf)
        hb, cb = one(1, S - 1 - s, hb, cb)
        return hf, cf, hb, cb

    zero = jnp.zeros((G * R, H), F32)
    start = (zero.astype(BF), zero, zero.astype(BF), zero)
    lax.fori_loop(0, S, step, start, unroll=shape.unroll)


def lstm_scan_back(shape, z, dh, c_ref, wrt):
    G, S, R = shape.groups, shape.steps, shape.rows

    def one(d, t, rec_hidden, rec_memory):
        def take(ref, at, lanes):
            at = pl.multiple_of(at, 8)
            return jnp.concatenate([ref[g, pl.ds(at, R), lanes] for g in range(G)], 0)

        lanes = slice(d * H, (d + 1) * H)
        at = pl.multiple_of(t * R, 8)
        zt = jnp.concatenate([z[d, g, pl.ds(at, R), :] for g in range(G)], 0)
        sig_i, sig_f, tan_g, sig_o = gate_acts(zt)
        tan_c = jnp.tanh(take(c_ref, t * R + R, lanes))
        before = take(c_ref, t * R + 2 * R * d, lanes)
        grad_h = take(dh, t * R, lanes) + rec_hidden
        grad_c = rec_memory + grad_h * (sig_o * (1.0 - tan_c * tan_c))
        grad_pre = jnp.concatenate(
            [
                grad_c * (tan_g * sig_i * (1.0 - sig_i)),
                grad_c * (before * sig_f * (1.0 - sig_f)),
                grad_c * (sig_i * (1.0 - tan_g * tan_g)),
                grad_h * (tan_c * sig_o * (1.0 - sig_o)),
            ],
            -1,
        ).astype(BF)
        full = grad_pre.astype(F32)
        for g in range(G):
            z[d, g, pl.ds(at, R), :] = full[g * R : (g + 1) * R]
        return dot(grad_pre, wrt[d]), grad_c * sig_f

    def step(s, carry):
        hf, cf, hb, cb = carry
        hf, cf = one(0, S - 1 - s, hf, cf)
        hb, cb = one(1, s, hb, cb)
        return hf, cf, hb, cb

    zero = jnp.zeros((G * R, H), F32)
    lax.fori_loop(0, S, step, (zero,) * 4, unroll=shape.unroll)


def branch_pregates(shape, xs, wi, bias, pg):
    def fill(g, i, r0):
        x = xs[g, pl.ds(r0, shape.crows), :].astype(BF)
        for d in range(2):
            pg[d, g, pl.ds(r0, shape.crows), :] = dot(x, wi[d]) + bias[d]

    chunk_loop(shape, fill)


def branch_back(shape, grads, xs, h_ref, c_ref, weights, vecs, turned_out, out, scratch):
    gi, gr = weights
    wi, wr, wit, wrt, wot, z, dh = scratch
    n, R = shape.crows, shape.rows
    forward_weights(gi, gr, wi, wr)
    for d in range(2):
        wit[d] = jnp.transpose(gi[0, d]).astype(BF)
        wrt[d] = jnp.transpose(gr[0, d]).astype(BF)
    wot[...] = turned_out.astype(BF)
    out[...] = jnp.zeros_like(out)
    bias, (o_bias, gain, _) = vecs

    def earlier(g, r0, d):
        at = pl.multiple_of(r0 + 2 * R * d, 8)
        return h_ref[g, pl.ds(at, n), d * H : (d + 1) * H].astype(BF)

    def first(g, i, r0):
        now = h_ref[g, pl.ds(pl.multiple_of(r0 + R, 8), n), :].astype(BF)
        unit, scale = norm_parts(dot_turned(now, wot[...]) + o_bias)
        grad = grads(g, i, r0)
        low = norm_back(grad, unit, scale, gain).astype(BF)
        dh[g, pl.ds(r0, n), :] = dot(low, wot[...])
        turned = dot_rows(low, now)
        for j in range(2):
            at = ROWS_MAPS + j * B
            out[at : at + B] += turned[:, j * LANES : (j + 1) * LANES]
        for j, value in enumerate((low.astype(F32), grad * unit, grad)):
            at = ROWS_VECS + 8 + j
            out[at : at + 1, :B] += jnp.sum(value, 0, keepdims=True)
        x = xs[g, pl.ds(r0, n), :].astype(BF)
        for d in range(2):
            z[d, g, pl.ds(r0, n), :] = dot(earlier(g, r0, d), wr[d]) + dot(x, wi[d]) + bias[d]

    chunk_loop(shape, first)
    lstm_scan_back(shape, z, dh, c_ref, wrt)

    def last(use):
        def fn(g, i, r0):
            x = xs[g, pl.ds(r0, n), :].astype(BF)
            total = None
            for d in range(2):
                full = z[d, g, pl.ds(r0, n), :]
                low = full.astype(BF)
                grad_in = dot_rows(x, low)
                grad_rec = dot_rows(earlier(g, r0, d), low)
                grad_bias = jnp.sum(full, 0, keepdims=True)
                for j in range(4):
                    lanes = slice(j * LANES, (j + 1) * LANES)
                    at = j * 384 + d * B
                    out[at : at + B] += grad_in[:, lanes]
                    at = j * 384 + 128 + d * H
                    out[at : at + H] += grad_rec[:, lanes]
                    at = ROWS_VECS + 4 * d + j
                    out[at : at + 1] += grad_bias[:, lanes]
                part = dot(low, wit[d])
                total = part if total is None else total + part
            use(g, i, r0, total)

        chunk_loop(shape, fn)

    return last


def back_scratch(shape):
    return [
        pltpu.VMEM((2, B, 4 * H), BF),
        pltpu.VMEM((2, H, 4 * H), BF),
        pltpu.VMEM((2, 4 * H, B), BF),
        pltpu.VMEM((2, 4 * H, H), BF),
        pltpu.VMEM((B, 2 * H), BF),
        pltpu.VMEM((2, shape.groups, shape.size, 4 * H), F32),
        pltpu.VMEM((shape.groups, shape.size, 2 * H), F32),
    ]


def packed(value, RP):
    rest = value[RP:]
    if rest.shape[0] < RP:
        rest = jnp.concatenate([rest, jnp.zeros((RP - rest.shape[0], B), F32)], 0)
    return jnp.concatenate([value[:RP], rest], 1).astype(BF)


def send_tiles(res, send, nb, RI):
    RP = send.shape[2]
    for d in range(nb):
        for c in range(TILES):
            send[d, c] = packed(res[c, d * RI : (d + 1) * RI], RP)


def add_tiles(res, back, nb, RI, lim):
    RP = back.shape[2]
    for d in range(nb):
        for c in range(TILES):
            both = back[d, c].astype(F32)
            for lo, hi, value in (
                (0, RP, both[:, :B]),
                (RP, RI, both[:, B:]),
            ):
                lo, hi = d * RI + lo, min(d * RI + hi, K * M)
                if lo >= hi:
                    continue
                mask = live(lim, c * HOP + lo // M, (hi - lo) // M)
                res[c, lo:hi] = (res[c, lo:hi] + value[: hi - lo]) * mask


def unpack_steps(rows, xs, T, RI):
    RP = rows.shape[1]

    def widen(t, _):
        both = rows[t].astype(F32)
        xs[0, pl.ds(pl.multiple_of(t * RI, 8), RP), :] = both[:, :B]
        if RI > RP:
            xs[0, pl.ds(pl.multiple_of(t * RI + RP, 8), RI - RP), :] = both[: RI - RP, B:]
        return 0

    lax.fori_loop(0, T, widen, 0, unroll=4 if T % 4 == 0 else 1)


def windows_of(mix, following, win):
    last = FRAMES + HOP + 1
    for i in range(1, BLOCKS):
        at = STRIDE * (i - 1)
        if at + 2 * STRIDE <= FRAMES * STRIDE:
            win[i * M : (i + 1) * M] = mix[:, at : at + 2 * STRIDE]
        elif at < FRAMES * STRIDE:
            win[i * M : (i + 1) * M] = jnp.concatenate([mix[:, at:], following[0, :, :STRIDE]], 1)
        elif i <= last:
            at -= FRAMES * STRIDE
            win[i * M : (i + 1) * M] = following[0, :, at : at + 2 * STRIDE]
        else:
            win[i * M :] = jnp.zeros(((BLOCKS - i) * M, 2 * STRIDE), F32)
            break


def softplus(value):
    return jnp.maximum(value, 0.0) + jnp.log1p(jnp.exp(-jnp.abs(value)))


def turned_out(proj, index):
    return proj[:, index * 2 * H : (index + 1) * 2 * H]


def intra_forward(shape, index, res, lim, gi, gr, vectors, proj, x_out, h_out, c_out, scratch):
    wi, wr, pg = scratch
    forward_weights(gi, gr, wi, wr)
    bias, (o_bias, gain, beta) = branch_vectors(vectors, index)
    n = shape.crows

    def keep(g, i, r0):
        x_out[g, pl.ds(pl.multiple_of(r0, 16), n), :] = res[g, pl.ds(r0, n), :].astype(BF)

    chunk_loop(shape, keep)
    branch_pregates(shape, res, wi, bias, pg)
    lstm_scan(shape, pg, wr, h_out, c_out)
    low_out = turned_out(proj, index).astype(BF)

    def close(g, i, r0):
        now = h_out[g, pl.ds(pl.multiple_of(r0 + shape.rows, 8), n), :].astype(BF)
        unit, _ = norm_parts(dot_turned(now, low_out) + o_bias)
        mask = live(lim, g * HOP + i * shape.chunk, shape.chunk)
        res[g, pl.ds(r0, n), :] = (res[g, pl.ds(r0, n), :] + (unit * gain + beta)) * mask

    chunk_loop(shape, close)


def zero_tail(res, c):
    if res.shape[1] > K * M:
        res[c, K * M :] = jnp.zeros((res.shape[1] - K * M, B), F32)


def first_kernel(shape, nb, RI, mix, following, leading, lengths, proj, vectors, gi, gr, res, send, x_out, h_out, c_out, win, wi, wr, pg, flat, bottle):
    lim = limits(lengths)
    flat[:M] = jnp.concatenate([leading[...], mix[:, :STRIDE]], 1)
    windows_of(mix, following, flat)
    win[...] = flat[...].astype(BF)
    w_enc = proj[:, BASE + N + B : BASE + N + B + 2 * STRIDE].astype(BF)
    w_bn = proj[:, BASE : BASE + N].astype(BF)
    gain, beta, b_bias = (pieces(vectors, j, 1) for j in range(3))
    for i in range(BLOCKS * M // CHUNK):
        at = i * CHUNK
        pre = dot_turned(win[at : at + CHUNK], w_enc)
        unit, _ = norm_parts(softplus(pre))
        normed = (unit * gain + beta).astype(BF)
        mask = live(lim, i * (CHUNK // M) - 1, CHUNK // M)
        bottle[at : at + CHUNK] = (dot_turned(normed, w_bn) + b_bias) * mask
    for c in range(TILES):
        res[c, : K * M] = bottle[(c * HOP + 1) * M : (c * HOP + 1 + K) * M]
        zero_tail(res, c)
    intra_forward(shape, 0, res, lim, gi, gr, vectors, proj, x_out, h_out, c_out, (wi, wr, pg))
    send_tiles(res, send, nb, RI)


def third_kernel(shape, nb, RI, res_in, back, lengths, proj, vectors, gi, gr, res, send, x_out, h_out, c_out, wi, wr, pg):
    lim = limits(lengths)
    res[...] = res_in[...]
    add_tiles(res, back, nb, RI, lim)
    intra_forward(shape, 2, res, lim, gi, gr, vectors, proj, x_out, h_out, c_out, (wi, wr, pg))
    send_tiles(res, send, nb, RI)


def inter_kernel(shape, RI, index, rows, proj, vectors, gi, gr, normed, h_out, c_out, wi, wr, pg, xs):
    forward_weights(gi, gr, wi, wr)
    unpack_steps(rows, xs, shape.steps, RI)
    bias, (o_bias, gain, beta) = branch_vectors(vectors, index)
    branch_pregates(shape, xs, wi, bias, pg)
    lstm_scan(shape, pg, wr, h_out, c_out)
    low_out = turned_out(proj, index).astype(BF)
    RP = normed.shape[1]

    def close(g, i, r0):
        now = h_out[g, pl.ds(pl.multiple_of(r0 + RI, 8), shape.crows), :].astype(BF)
        unit, _ = norm_parts(dot_turned(now, low_out) + o_bias)
        value = unit * gain + beta
        for j in range(shape.chunk):
            normed[i * shape.chunk + j] = packed(value[j * RI : (j + 1) * RI], RP)

    chunk_loop(shape, close)


EDGE = (HOP + 1) * M
EDGE_TOP = 208


def edge_pack(value):
    rest = jnp.concatenate([value[EDGE_TOP:], jnp.zeros((2 * EDGE_TOP - EDGE, B), F32)], 0)
    return jnp.concatenate([value[:EDGE_TOP], rest], 1)


def edge_unpack(ref):
    return jnp.concatenate([ref[:, :B], ref[: EDGE - EDGE_TOP, B:]], 0)


def part_kernel(nb, RI, res_in, back, lengths, part, up, down, res):
    res[...] = res_in[...]
    add_tiles(res, back, nb, RI, limits(lengths))
    half = HOP * M
    part[:half] = res[0, :half]
    for c in range(1, TILES):
        part[c * half : (c + 1) * half] = res[c, :half] + res[c - 1, half : 2 * half]
    part[TILES * half :] = res[TILES - 1, half : 2 * half]
    up[...] = edge_pack(part[TILES * half - M :])
    down[...] = edge_pack(part[: half + M])


def middle_kernel(nb, RI, part, before, after, lengths, win, goal, following, proj, vectors, send, gres, genc, gm, feats, dec, tgt, gest, enc, gate, src, act):
    lim = limits(lengths)
    half = HOP * M
    top = M + TILES * half
    total = BLOCKS * M
    early, late = edge_unpack(before), edge_unpack(after)
    feats[:M] = early[:M]
    feats[M : M + half] = part[:half] + early[M:]
    feats[M + half : top] = part[half : TILES * half]
    feats[top : top + half] = part[TILES * half :] + late[:half]
    feats[top + half : top + half + M] = late[half:]
    feats[top + half + M :] = jnp.zeros((PADDED * M - top - half - M, B), F32)
    low_mask = proj[:, BASE + N : BASE + N + B].astype(BF)
    w_enc = proj[:, BASE + N + B : BASE + N + B + 2 * STRIDE].astype(BF)
    low_dec = proj[:, BASE + N + B + 2 * STRIDE : BASE + N + B + 4 * STRIDE].astype(BF)
    m_bias = pieces(vectors, vectors.shape[0] * 2 - 1, 1)
    root = 0.7978845608028654
    cube = 0.044715
    dec[total:] = jnp.zeros((PADDED * M - total, 2 * STRIDE), F32)
    for i in range(total // CHUNK):
        rows = slice(i * CHUNK, (i + 1) * CHUNK)
        x = feats[rows]
        low = (0.5 * x * (1.0 + jnp.tanh(root * (x + cube * x * x * x)))).astype(BF)
        encoded = softplus(dot_turned(win[rows], w_enc))
        mask = 0.5 * jnp.tanh(0.5 * (dot_turned(low, low_mask) + m_bias)) + 0.5
        source = (mask * encoded).astype(BF)
        enc[rows] = encoded
        gate[rows] = mask
        src[rows] = source.astype(F32)
        act[rows] = low.astype(F32)
        dec[rows] = dot(source, low_dec)
    dec[:M] = dec[:M] * jnp.where(lax.axis_index("block") > 0, 1.0, 0.0)
    for ref in (enc, gate, src, act):
        ref[total:] = jnp.zeros((PADDED * M - total, B), F32)
    for i in range(1, FRAMES + 1):
        tgt[i * M : (i + 1) * M] = goal[:, STRIDE * (i - 1) : STRIDE * i]
    for i in range(FRAMES + 1, FRAMES + HOP + 2):
        at = STRIDE * (i - 1 - FRAMES)
        tgt[i * M : (i + 1) * M] = following[1, :, at : at + STRIDE]
    tgt[(FRAMES + HOP + 2) * M :] = jnp.zeros(((PADDED - FRAMES - HOP - 2) * M, STRIDE), F32)
    estimate = dec[M:total, :STRIDE] + dec[: total - M, STRIDE:]
    count = BLOCKS - 1
    spot = lax.broadcasted_iota(jnp.int32, (count, M, STRIDE), 0)
    phase = lax.broadcasted_iota(jnp.int32, (count, M, STRIDE), 2)
    near = spot < FRAMES + HOP + 1
    valid = jnp.where(near & (spot * STRIDE + phase < lim[:, :STRIDE][None]), 1.0, 0.0)
    inside = jnp.where(spot < FRAMES, valid, 0.0).reshape(count * M, STRIDE)
    valid = valid.reshape(count * M, STRIDE)
    error = estimate - tgt[M:total]
    smoothed = jnp.sqrt(error * error + 1.0)
    gest[:M] = jnp.zeros((M, STRIDE), F32)
    gest[M:total] = valid * error / smoothed
    gest[total:] = jnp.zeros((PADDED * M - total, STRIDE), F32)
    loss = jnp.sum(jnp.sum(inside * (smoothed - 1.0), 0, keepdims=True), 1, keepdims=True)
    seen = jnp.sum(jnp.sum(inside, 0, keepdims=True), 1, keepdims=True)
    gm[...] = jnp.zeros_like(gm)
    gm[132:133] = jnp.broadcast_to(loss, (1, LANES))
    gm[133:134] = jnp.broadcast_to(seen, (1, LANES))
    for i in range(total // CHUNK):
        at = i * CHUNK + M
        rows = slice(at, at + CHUNK)
        grad_dec = jnp.concatenate([gest[rows], gest[at + M : at + M + CHUNK]], 1).astype(BF)
        mine = own(i * (CHUNK // M), CHUNK // M)
        mine_low = mine.astype(BF)
        gm[64:128, 16:32] += dot_rows(src[rows].astype(BF) * mine_low, grad_dec)
        grad_source = dot_turned(grad_dec, low_dec)
        mask = gate[rows]
        grad_logit = (grad_source * enc[rows] * mask * (1.0 - mask)).astype(BF)
        enc[rows] = grad_source * mask
        gm[:64, 64:] += dot_rows(grad_logit * mine_low, act[rows].astype(BF))
        gm[131:132, :B] += jnp.sum(grad_logit.astype(F32) * mine, 0, keepdims=True)
        x = feats[rows]
        curve = jnp.tanh(root * (x + cube * x * x * x))
        slope = 0.5 * (1.0 + curve) + (0.5 * root) * x * (1.0 - curve * curve) * (
            1.0 + (3.0 * cube) * x * x
        )
        feats[rows] = slope * dot(grad_logit, low_mask)
    genc[...] = enc[M : M + FRAMES * M]
    for c in range(TILES):
        gres[c, : K * M] = feats[M + c * half : M + c * half + K * M] * live(lim, c * HOP, K)
        zero_tail(gres, c)
    send_tiles(gres, send, nb, RI)


def inter_back_kernel(shape, RI, index, grad_rows, rows, h_ref, c_ref, proj, vectors, gi, gr, send, out, *scratch):
    xs, gs, core = scratch[0], scratch[1], scratch[2:]
    unpack_steps(rows, xs, shape.steps, RI)
    unpack_steps(grad_rows, gs, shape.steps, RI)
    RP = send.shape[1]

    def grads(g, i, r0):
        return gs[g, pl.ds(r0, shape.crows), :]

    last = branch_back(
        shape, grads, xs, h_ref, c_ref, (gi, gr), branch_vectors(vectors, index), turned_out(proj, index), out, core
    )

    def use(g, i, r0, total):
        for j in range(shape.chunk):
            send[i * shape.chunk + j] = packed(total[j * RI : (j + 1) * RI], RP)

    last(use)


def intra_back(shape, index, gres, x_ref, h_ref, c_ref, proj, vectors, gi, gr, out, core):
    n = shape.crows

    def grads(g, i, r0):
        return gres[g, pl.ds(r0, n), :]

    last = branch_back(
        shape, grads, x_ref, h_ref, c_ref, (gi, gr), branch_vectors(vectors, index), turned_out(proj, index), out, core
    )

    def use(g, i, r0, total):
        gres[g, pl.ds(r0, n), :] = gres[g, pl.ds(r0, n), :] + total

    last(use)


def third_back_kernel(shape, nb, RI, gres_in, back, lengths, x_ref, h_ref, c_ref, proj, vectors, gi, gr, gres, send, out, *core):
    lim = limits(lengths)
    gres[...] = gres_in[...]
    add_tiles(gres, back, nb, RI, lim)
    intra_back(shape, 2, gres, x_ref, h_ref, c_ref, proj, vectors, gi, gr, out, core)
    for c in range(TILES):
        gres[c, : K * M] = gres[c, : K * M] * live(lim, c * HOP, K)
    send_tiles(gres, send, nb, RI)


def first_back_kernel(shape, nb, RI, gres_in, back, lengths, x_ref, h_ref, c_ref, proj, vectors, gi, gr, win, genc, gm_in, out, gres, bottle, *core):
    lim = limits(lengths)
    gres[...] = gres_in[...]
    add_tiles(gres, back, nb, RI, lim)
    intra_back(shape, 0, gres, x_ref, h_ref, c_ref, proj, vectors, gi, gr, out, core)
    gm = ROWS_G
    out[gm : gm + gm_in.shape[0]] = gm_in[...]
    bottle[...] = jnp.zeros_like(bottle)
    for c in range(TILES):
        at = (c * HOP + 1) * M
        bottle[at : at + K * M] += gres[c, : K * M]
    w_enc = proj[:, BASE + N + B : BASE + N + B + 2 * STRIDE].astype(BF)
    w_bn = proj[:, BASE : BASE + N].astype(BF)
    gain, beta = (pieces(vectors, j, 1) for j in range(2))
    own_rows = FRAMES * M
    for i in range(BLOCKS * M // CHUNK):
        at = i * CHUNK
        rows = slice(at, at + CHUNK)
        pre = dot_turned(win[rows], w_enc)
        unit, scale = norm_parts(softplus(pre))
        normed = (unit * gain + beta).astype(BF)
        low = (bottle[rows] * live(lim, i * (CHUNK // M) - 1, CHUNK // M)).astype(BF)
        out[gm : gm + 64, :N] += dot_rows(low, normed)
        grad_normed = dot(low, w_bn)
        for j, value in enumerate((grad_normed * unit, grad_normed, low.astype(F32))):
            out[gm + 128 + j : gm + 129 + j, :B] += jnp.sum(value, 0, keepdims=True)
        grad_enc = norm_back(grad_normed, unit, scale, gain)
        lo, hi = max(at - M, 0), min(at + CHUNK - M, own_rows)
        if lo < hi:
            piece = genc[lo:hi]
            above, below = lo + M - at, at + CHUNK - M - hi
            if above:
                piece = jnp.concatenate([jnp.zeros((above, B), F32), piece], 0)
            if below:
                piece = jnp.concatenate([piece, jnp.zeros((below, B), F32)], 0)
            grad_enc = grad_enc + piece
        grad_pre = (grad_enc * (0.5 * jnp.tanh(0.5 * pre) + 0.5)).astype(BF)
        out[gm + 64 : gm + 128, :16] += dot_rows(grad_pre, win[rows])


def adam_parts(grad, moment, square, weight, average, decay):
    moment = BETA_ONE * moment + (1.0 - BETA_ONE) * grad
    square = BETA_TWO * square + (1.0 - BETA_TWO) * grad * grad
    corrected = moment * (1.0 / (1.0 - BETA_ONE**STEP))
    scaled = square * (1.0 / (1.0 - BETA_TWO**STEP))
    weight = weight - RATE * (corrected / (jnp.sqrt(scaled) + ADAM_EPS) + decay * weight)
    average = KEEP * average + (1.0 - KEEP) * weight
    return moment, square, weight, average, weight.astype(BF)


def adam_kernel(*refs):
    gs, old = refs[:4], refs[4:20]
    scalars, new = refs[20], refs[21:41]
    gv = refs[41]
    first = gs[0]
    gm = ROWS_G
    gv[:1] = jnp.concatenate([first[gm + 128 : gm + 129, :N], first[gm + 129 : gm + 130, :N]], 1)
    gv[1:2, :N] = first[gm + 130 : gm + 131, :N]
    gv[gv.shape[0] - 1 :, N:] = first[gm + 131 : gm + 132, :N]
    for r in range(4):
        at = 3 + 19 * r
        for j in range(8):
            row = gs[r][ROWS_VECS + j : ROWS_VECS + j + 1]
            for k in range(2):
                q = at + 2 * j + k
                gv[q // 2 : q // 2 + 1, (q % 2) * N : (q % 2 + 1) * N] = row[:, k * N : (k + 1) * N]
        for j in range(3):
            q = at + 16 + j
            gv[q // 2 : q // 2 + 1, (q % 2) * N : (q % 2 + 1) * N] = gs[r][ROWS_VECS + 8 + j : ROWS_VECS + 9 + j, :N]
    part = jnp.zeros((8, LANES), F32)
    for r in range(4):
        value = gs[r][:ROWS_VECS].reshape(ROWS_VECS // 8, 8, LANES)
        part = part + jnp.sum(value * value, 0)
    value = first[gm : gm + 128].reshape(16, 8, LANES)
    part = part + jnp.sum(value * value, 0)
    value = gv[...].reshape(5, 8, LANES)
    part = part + jnp.sum(value * value, 0)
    squared = jnp.sum(jnp.sum(part, 0, keepdims=True), 1, keepdims=True)
    loss, count = first[gm + 132 : gm + 133, :1], first[gm + 133 : gm + 134, :1]
    norm = jnp.sqrt(squared) / count
    factor = jnp.minimum(1.0, CLIP / norm) / count
    row = lax.broadcasted_iota(jnp.int32, (8, LANES), 0)
    scalars[...] = jnp.where(row == 0, loss, jnp.where(row == 1, count, norm))

    def update(kind, index, grad, decay):
        results = adam_parts(
            grad * factor,
            old[4 + kind][index],
            old[8 + kind][index],
            old[kind][index],
            old[12 + kind][index],
            decay,
        )
        for j, value in enumerate(results):
            new[4 * j + kind][index] = value

    for r in range(4):
        for d in range(2):
            for j in range(4):
                lanes = slice(j * LANES, (j + 1) * LANES)
                at = j * 384 + d * B
                update(0, (r, d, slice(None), lanes), gs[r][at : at + B], DECAY)
                at = j * 384 + 128 + d * H
                update(1, (r, d, slice(None), lanes), gs[r][at : at + H], DECAY)
        for j in range(2):
            at = ROWS_MAPS + j * B
            lanes = slice(r * 2 * H + j * LANES, r * 2 * H + (j + 1) * LANES)
            update(2, (slice(None), lanes), gs[r][at : at + B], DECAY)
    update(2, (slice(None), slice(BASE, BASE + LANES)), first[gm : gm + 64], DECAY)
    update(2, (slice(None), slice(BASE + LANES, BASE + LANES + 32)), first[gm + 64 : gm + 128, :32], DECAY)
    update(3, (slice(None), slice(None)), gv[...], 0.0)


def call(kernel, outs, ins, scratch, index=None, limit=56, micros=20):
    vmem = pl.BlockSpec(memory_space=pltpu.VMEM)
    specs = [
        pl.BlockSpec(memory_space=pltpu.SMEM) if a.ndim == 1 and a.dtype == jnp.int32 else vmem
        for a in ins
    ]
    extra = []
    wrapped = kernel
    if index is not None:
        big = [i for i, a in enumerate(ins) if a.ndim == 4 and a.shape[:2] == (2 * LAYERS, 2)]
        for i in big:
            specs[i] = pl.BlockSpec(memory_space=pl.ANY)
        extra = [pltpu.VMEM((1,) + ins[i].shape[1:], F32) for i in big]
        extra.append(pltpu.SemaphoreType.DMA((len(big),)))

        def wrapped(*refs):
            refs = list(refs)
            held, sem = refs[len(refs) - len(extra) : -1], refs[-1]
            copies = []
            for j, i in enumerate(big):
                copies.append(pltpu.make_async_copy(refs[i].at[pl.ds(index, 1)], held[j], sem.at[j]))
                copies[-1].start()
            for copy in copies:
                copy.wait()
            for j, i in enumerate(big):
                refs[i] = held[j]
            kernel(*refs[: len(refs) - len(extra)])

    return pl.pallas_call(
        wrapped,
        out_shape=outs,
        in_specs=specs,
        out_specs=[vmem] * len(outs),
        scratch_shapes=list(scratch) + extra,
        compiler_params=pltpu.CompilerParams(vmem_limit_bytes=limit * 1024 * 1024),
        cost_estimate=pl.CostEstimate(
            flops=micros * 10**9, bytes_accessed=micros * 10**6, transcendentals=0
        ),
    )(*ins)


def shift(block, axis, distance):
    size = lax.axis_size(axis)
    route = [(i, i + distance) for i in range(size) if 0 <= i + distance < size]
    return lax.ppermute(block, axis, route)


def exchange(block):
    return lax.all_to_all(block, "block", split_axis=0, concat_axis=0, tiled=True)


def flip(block, bit):
    size = lax.axis_size("dp")
    return lax.ppermute(block, "dp", [(i, i ^ (1 << bit)) for i in range(size)])


def bits():
    return lax.axis_size("dp").bit_length() - 1


def halve(block):
    for bit in range(bits()):
        half = block.shape[0] // 2
        mine = (lax.axis_index("dp") >> bit) & 1
        given = lax.dynamic_slice_in_dim(block, (1 - mine) * half, half, 0)
        block = lax.dynamic_slice_in_dim(block, mine * half, half, 0) + flip(given, bit)
    return block


def double(block):
    for bit in reversed(range(bits())):
        mine = (lax.axis_index("dp") >> bit) & 1
        other = flip(block, bit)
        block = jnp.where(
            mine == 0, jnp.concatenate([block, other], 0), jnp.concatenate([other, block], 0)
        )
    return block


def scatter_sum(block):
    nb = lax.axis_size("block")
    block = halve(block)
    rows = block.shape[0]
    part = -(-rows // (8 * nb)) * 8
    if part * nb > rows:
        block = jnp.concatenate([block, jnp.zeros((part * nb - rows, LANES), F32)], 0)
    return jnp.sum(exchange(block.reshape(nb, part, LANES)), 0)


def gather_sums(parts, sizes):
    nb, dp = lax.axis_size("block"), lax.axis_size("dp")
    mine = jnp.concatenate(parts, 0)
    all_parts = exchange(jnp.broadcast_to(mine[None], (nb,) + mine.shape))
    given, at = [], 0
    for part, size in zip(parts, sizes):
        rows = part.shape[0]
        block = all_parts[:, at : at + rows].reshape(nb * rows, LANES)
        given.append(double(block[: size // dp]))
        at += rows
    return given


def body(
    mixture,
    target,
    lengths,
    input_gates,
    recur_gates,
    projections,
    vectors,
    moment_input,
    moment_recur,
    moment_proj,
    moment_vecs,
    square_input,
    square_recur,
    square_proj,
    square_vecs,
    average_input,
    average_recur,
    average_proj,
    average_vecs,
):
    nb = lax.axis_size("block")
    RI = -(-K // nb) * M
    intra = Shape(TILES, K, M)
    inter = Shape(1, TILES * nb, RI)
    T = inter.steps
    gi, gr = input_gates, recur_gates
    proj = projections.T
    vectors_wide = vectors.reshape(-1, LANES)
    reach = (HOP + 2) * STRIDE
    following = shift(jnp.stack([mixture[:, :reach], target[:, :reach]]), "block", -1)
    leading = shift(mixture[:, -STRIDE:], "block", 1)

    RP = -(-RI // 16) * 8
    res_shape = SDS((TILES, nb * RI, B), F32)
    send_shape = SDS((nb, TILES, RP, 2 * B), BF)
    steps_shape = SDS((T, RP, 2 * B), BF)
    x_shape = SDS((TILES, K * M, B), BF)

    def state(shape):
        return SDS((shape.groups, shape.wide, 2 * H), F32)

    def fwd_scratch(shape):
        return [
            pltpu.VMEM((2, B, 4 * H), BF),
            pltpu.VMEM((2, H, 4 * H), BF),
            pltpu.VMEM((2, shape.groups, shape.size, 4 * H), F32),
        ]

    res0, send, x0, h0, c0, win = call(
        functools.partial(first_kernel, intra, nb, RI),
        [res_shape, send_shape, x_shape, state(intra), state(intra), SDS((BLOCKS * M, 2 * STRIDE), BF)],
        [mixture, following, leading, lengths, proj, vectors_wide, gi, gr],
        fwd_scratch(intra)
        + [pltpu.VMEM((BLOCKS * M, 2 * STRIDE), F32), pltpu.VMEM((BLOCKS * M, B), F32)],
        0,
    )

    def inter_step(send, index):
        rows = exchange(send).reshape(T, RP, 2 * B)
        normed, h, c = call(
            functools.partial(inter_kernel, inter, RI, index),
            [steps_shape, state(inter), state(inter)],
            [rows, proj, vectors_wide, gi, gr],
            fwd_scratch(inter) + [pltpu.VMEM((1, inter.size, B), F32)],
            index,
        )
        return rows, h, c, exchange(normed.reshape(send_shape.shape))

    rows1, h1, c1, back = inter_step(send, 1)
    res2, send, x2, h2, c2 = call(
        functools.partial(third_kernel, intra, nb, RI),
        [res_shape, send_shape, x_shape, state(intra), state(intra)],
        [res0, back, lengths, proj, vectors_wide, gi, gr],
        fwd_scratch(intra),
        2,
    )
    rows3, h3, c3, back = inter_step(send, 3)
    edge_shape = SDS((EDGE_TOP, 2 * B), F32)
    part, up, down = call(
        functools.partial(part_kernel, nb, RI),
        [SDS(((FRAMES + HOP) * M, B), F32), edge_shape, edge_shape],
        [res2, back, lengths],
        [pltpu.VMEM(res_shape.shape, F32)],
    )
    before = shift(up, "block", 1)
    after = shift(down, "block", -1)
    tall = PADDED * M
    send, gres, genc, gm = call(
        functools.partial(middle_kernel, nb, RI),
        [send_shape, res_shape, SDS((FRAMES * M, B), F32), SDS((136, LANES), F32)],
        [part, before, after, lengths, win, target, following, proj, vectors_wide],
        [
            pltpu.VMEM((tall, B), F32),
            pltpu.VMEM((tall, 2 * STRIDE), F32),
            pltpu.VMEM((tall, STRIDE), F32),
            pltpu.VMEM((tall, STRIDE), F32),
            pltpu.VMEM((tall, B), F32),
            pltpu.VMEM((tall, B), F32),
            pltpu.VMEM((tall, B), F32),
            pltpu.VMEM((tall, B), F32),
        ],
    )
    out_shape = SDS((ROWS_G, LANES), F32)

    def inter_back(send, rows, h, c, index):
        grad_rows = exchange(send).reshape(T, RP, 2 * B)
        send, out = call(
            functools.partial(inter_back_kernel, inter, RI, index),
            [steps_shape, out_shape],
            [grad_rows, rows, h, c, proj, vectors_wide, gi, gr],
            [pltpu.VMEM((1, inter.size, B), F32)] * 2 + back_scratch(inter),
            index,
        )
        return exchange(send.reshape(send_shape.shape)), out

    back, out3 = inter_back(send, rows3, h3, c3, 3)
    gres, send, out2 = call(
        functools.partial(third_back_kernel, intra, nb, RI),
        [res_shape, send_shape, out_shape],
        [gres, back, lengths, x2, h2, c2, proj, vectors_wide, gi, gr],
        back_scratch(intra),
        2,
    )
    back, out1 = inter_back(send, rows1, h1, c1, 1)
    (out0,) = call(
        functools.partial(first_back_kernel, intra, nb, RI),
        [SDS((ROWS_FIRST, LANES), F32)],
        [gres, back, lengths, x0, h0, c0, proj, vectors_wide, gi, gr, win, genc, gm],
        [pltpu.VMEM(res_shape.shape, F32), pltpu.VMEM((BLOCKS * M, B), F32)] + back_scratch(intra),
        0,
    )
    sums = gather_sums([scatter_sum(out0), scatter_sum(out1)], [ROWS_FIRST, ROWS_G])
    sums += gather_sums([scatter_sum(out2), scatter_sum(out3)], [ROWS_G, ROWS_G])
    old = [
        input_gates, recur_gates, projections, vectors,
        moment_input, moment_recur, moment_proj, moment_vecs,
        square_input, square_recur, square_proj, square_vecs,
        average_input, average_recur, average_proj, average_vecs,
    ]
    for i in range(2, 16, 4):
        old[i] = old[i].T
    for i in range(3, 16, 4):
        old[i] = old[i].reshape(-1, LANES)
    new = [SDS(a.shape, F32) for a in old[:4]] * 4 + [SDS(a.shape, BF) for a in old[:4]]
    scalars, *new = call(
        adam_kernel,
        [SDS((8, LANES), F32)] + new,
        sums + old,
        [pltpu.VMEM(old[3].shape, F32)],
    )
    for i in range(2, 20, 4):
        new[i] = new[i].T
    for i in range(3, 20, 4):
        new[i] = new[i].reshape(-1)
    return (scalars[0, 0], scalars[1, 0], scalars[2, 0], *new)


def solution(mesh):
    in_specs = (P("dp", "block"), P("dp", "block"), P("dp")) + (P(),) * 16
    return jax.shard_map(
        body, mesh=mesh, in_specs=in_specs, out_specs=(P(),) * 23, check_vma=False
    )
```

time: 574 us -> 452 us (0.79)
  blocking collectives: 164 us -> 71.4 us
  starting transfers between devices: 11 us -> 56 us
  local copies, waits for them, and re-layouts: 42.7 us -> 13.9 us
  waiting for transfers between devices: 99.9 us -> 78.8 us
  other arithmetic: 26.8 us -> 7.55 us
  between operations: 20.7 us -> 1.63 us
  Pallas kernels: 199 us -> 214 us
    psum x1 -> x0, waiting for transfers between devices: 93.5 us -> none  [body(): outs, gm_mid, gm_first = lax.psum((outs, gm_mid, gm_first), ('block', 'dp'))]
    all_to_all x0 -> x9, waiting for transfers between devices: none -> 58.4 us  [exchange(): lax.all_to_all(block, 'block', split_axis=0, concat_axis=0, tiled=True)]
    all_to_all x8 -> x5, blocking collectives: 124 us -> 71.4 us  [exchange(): lax.all_to_all(block, 'block', split_axis=0, concat_axis=0, tiled=True)]
    psum x1 -> x0, blocking collectives: 40.5 us -> none  [body(): outs, gm_mid, gm_first = lax.psum((outs, gm_mid, gm_first), ('block', 'dp'))]
    all_to_all x0 -> x9, starting transfers between devices: none -> 35.1 us  [exchange(): lax.all_to_all(block, 'block', split_axis=0, concat_axis=0, tiled=True)]
    pallas_call x10 -> x11, Pallas kernels: 199 us -> 214 us  [call(): pl.pallas_call(wrapped, out_shape=outs, in_specs=specs, out_specs=[vmem]...]
    ppermute x0 -> x16, waiting for transfers between devices: none -> 13.8 us  [flip(): return lax.ppermute(block, 'dp', [(i, i ^ 1 << bit) for i in range(size)])]
    ppermute x0 -> x16, starting transfers between devices: none -> 10 us  [flip(): return lax.ppermute(block, 'dp', [(i, i ^ 1 << bit) for i in range(size)])]
  transfers between devices with their start and end apart: 5 -> 29, of which waited for: 2 -> 14; matrix products, arithmetic and copies ran while one was open for 2% -> 3% of each run, Pallas kernels for 0% -> 20%
where the time goes in v1:
time: 452 us; the launch traced here: 444 us
  Pallas kernels  214 us (47%)
  waiting for transfers between devices  78.8 us (17%)
  blocking collectives  71.4 us (16%)
  starting transfers between devices  56 us (12%)
  local copies, waits for them, and re-layouts  13.9 us (3%)
  other arithmetic  7.55 us (2%)
    pallas_call x11, Pallas kernels, call(): pl.pallas_call(wrapped, out_shape=outs, in_specs=specs, out_specs=[vmem]...  214 us
    all_to_all x5, blocking collectives, exchange(): lax.all_to_all(block, 'block', split_axis=0, concat_axis=0, tiled=True)  71.4 us
    all_to_all x9, waiting for transfers between devices, exchange(): lax.all_to_all(block, 'block', split_axis=0, concat_axis=0, tiled=True)  58.4 us
    all_to_all x9, starting transfers between devices, exchange(): lax.all_to_all(block, 'block', split_axis=0, concat_axis=0, tiled=True)  35.1 us
    ppermute x16, waiting for transfers between devices, flip(): return lax.ppermute(block, 'dp', [(i, i ^ 1 << bit) for i in range(size)])  13.8 us
    ppermute x4, starting transfers between devices, shift(): return lax.ppermute(block, axis, route)  10.8 us
    ppermute x16, starting transfers between devices, flip(): return lax.ppermute(block, 'dp', [(i, i ^ 1 << bit) for i in range(size)])  10 us
  transfers between devices with their start and end apart: 29, of which 14 were waited for; matrix products, arithmetic and copies ran while one was open for 3% of the time, Pallas kernels for 20%

profile of v1, /device:TPU:0, one launch (start us, length us, event | category | flops | bytes accessed | tf_op | source)
XLA Modules:
  0.0 443.6 jit_solution(4843475426606701502)
XLA Ops:
  4.2 5.5 %collective-permute-start.1 = (f32[8,8]{1,0:T(8,128)S(1)}, f32[8,8]{1,0:T(8,128)S(1)}, u32[]{:S(2)}, u32[]{:S(2)}) collective-permute-start(f32[8,8]{1,0:T(8,128)S(1)} %slice.44), channel_id=1, source_target_pairs={{0,4},{4,8},{8,12},{12,16},{16,20},{20,24},{24,28},{1,5},{5,9},{9,... | collective-permute-start | bytes 776 | tf_op jit(solution)/shard_map/ppermute | solution.py:772
  11.6 26.5 %shard_map.362 = (f32[3,832,64]{2,1,0:T(8,128)}, bf16[8,3,56,128]{3,2,1,0:T(8,128)(2,1)}, bf16[3,800,64]{2,1,0:T(8,128)(2,1)}, f32[3,816,256]{2,1,0:T(8,128)}, f...) custom-call(f32[8,1200]{1,0:T(8,128)} %refs_0_.1, f32[2,8,416]{2,1,0:T(8,128)} %copy-done.8, f32[8,8]{1,0:T(8,128)} %copy-done.9, ...), custom_call_target="tpu_custom_call" | custom-call | flops 20000000000 | bytes 20000000 | tf_op jit(solution)/shard_map/pallas_call | solution.py:756
  38.1 17.8 %all_to_all.70 = bf16[8,3,56,128]{3,2,1,0:T(8,128)(2,1)} all-to-all(bf16[8,3,56,128]{3,2,1,0:T(8,128)(2,1)} %get-tuple-element.76), channel_id=1, replica_groups=mesh['block'=8,'dp'=4] {'block'}, dimensions={0} | all-to-all | bytes 688128 | tf_op jit(solution)/shard_map/all_to_all | solution.py:776
  55.9 14.0 %shard_map.363 = (bf16[24,56,128]{2,1,0:T(8,128)(2,1)}, f32[1,2704,256]{2,1,0:T(8,128)}, f32[1,2704,256]{2,1,0:T(8,128)}) custom-call(bf16[24,56,128]{2,1,0:T(8,128)(2,1)} %bitcast.45, f32[64,1184]{1,0:T(8,128)} %bitcast.56, f32[40,128]{1,0:T(8,128)} %bitcast.69, f32[4,2,64,512]{3,2,1,0:T(8,128)} %refs_4_.5, f32[4,2,128,512]{3,2,1,0:T(8,128)} %refs_5_.3), custom_call_target="tpu_custom_call" | custom-call | flops 20000000000 | bytes 20000000 | tf_op jit(solution)/shard_map/pallas_call | solution.py:756
  69.9 13.6 %all_to_all.71.refs_1_ = bf16[8,3,56,128]{3,2,1,0:T(8,128)(2,1)} all-to-all(bf16[8,3,56,128]{3,2,1,0:T(8,128)(2,1)} %bitcast.53), channel_id=1, replica_groups=mesh['block'=8,'dp'=4] {'block'}, dimensions={0} | all-to-all | bytes 688128 | tf_op jit(solution)/shard_map/all_to_all | solution.py:776
  83.5 25.6 %shard_map.364 = (f32[3,832,64]{2,1,0:T(8,128)}, bf16[8,3,56,128]{3,2,1,0:T(8,128)(2,1)}, bf16[3,800,64]{2,1,0:T(8,128)(2,1)}, f32[3,816,256]{2,1,0:T(8,128)}, f32[3,816,256]{2,1,0:T(8,128)}) custom-call(f32[3,832,64]{2,1,0:T(8,128)} %get-tuple-element.75.refs_0_, bf16[8,3,56,128]{3,2,1,0:T(8,128)(2,1)} %all_to_all.71.refs_1_, s32[8]{0:T(128)} %refs_2_.5, ...), custom_call_target="tpu_custom_call" | custom-call | flops 20000000000 | bytes 20000000 | tf_op jit(solution)/shard_map/pallas_call | solution.py:756
  109.1 13.4 %all_to_all.72 = bf16[8,3,56,128]{3,2,1,0:T(8,128)(2,1)} all-to-all(bf16[8,3,56,128]{3,2,1,0:T(8,128)(2,1)} %get-tuple-element.79), channel_id=1, replica_groups=mesh['block'=8,'dp'=4] {'block'}, dimensions={0} | all-to-all | bytes 688128 | tf_op jit(solution)/shard_map/all_to_all | solution.py:776
  122.5 14.0 %shard_map.365 = (bf16[24,56,128]{2,1,0:T(8,128)(2,1)}, f32[1,2704,256]{2,1,0:T(8,128)}, f32[1,2704,256]{2,1,0:T(8,128)}) custom-call(bf16[24,56,128]{2,1,0:T(8,128)(2,1)} %bitcast.48, f32[64,1184]{1,0:T(8,128)} %bitcast.58, f32[40,128]{1,0:T(8,128)} %bitcast.71, f32[4,2,64,512]{3,2,1,0:T(8,128)} %refs_4_.5, f32[4,2,128,512]{3,2,1,0:T(8,128)} %refs_5_.3), custom_call_target="tpu_custom_call" | custom-call | flops 20000000000 | bytes 20000000 | tf_op jit(solution)/shard_map/pallas_call | solution.py:756
  136.6 13.2 %all_to_all.73.back = bf16[8,3,56,128]{3,2,1,0:T(8,128)(2,1)} all-to-all(bf16[8,3,56,128]{3,2,1,0:T(8,128)(2,1)} %bitcast.54), channel_id=1, replica_groups=mesh['block'=8,'dp'=4] {'block'}, dimensions={0} | all-to-all | bytes 688128 | tf_op jit(solution)/shard_map/all_to_all | solution.py:776
  157.6 4.2 collective-permute-done.3.after
  162.5 6.0 %shard_map.367 = (bf16[8,3,56,128]{3,2,1,0:T(8,128)(2,1)}, f32[3,832,64]{2,1,0:T(8,128)}, f32[1200,64]{1,0:T(8,128)}, f32[136,128]{1,0:T(8,128)}) custom-call(f32[1600,64]{1,0:T(8,128)} %get-tuple-element.81.part, f32[208,128]{1,0:T(8,128)} %copy-done.6, f32[208,128]{1,0:T(8,128)} %copy-done.7, s32[8]{0:T(128)} %refs_2_.5, ...), custom_call_target="tpu_custom_call" | custom-call | flops 20000000000 | bytes 20000000 | tf_op jit(solution)/shard_map/pallas_call | solution.py:756
  168.5 13.4 %all_to_all.74 = bf16[8,3,56,128]{3,2,1,0:T(8,128)(2,1)} all-to-all(bf16[8,3,56,128]{3,2,1,0:T(8,128)(2,1)} %get-tuple-element.86), channel_id=1, replica_groups=mesh['block'=8,'dp'=4] {'block'}, dimensions={0} | all-to-all | bytes 688128 | tf_op jit(solution)/shard_map/all_to_all | solution.py:776
  181.9 22.5 %shard_map.368 = (bf16[24,56,128]{2,1,0:T(8,128)(2,1)}, f32[1696,128]{1,0:T(8,128)}) custom-call(bf16[24,56,128]{2,1,0:T(8,128)(2,1)} %bitcast.52, bf16[24,56,128]{2,1,0:T(8,128)(2,1)} %bitcast.49, f32[1,2704,256]{2,1,0:T(8,128)} %get-tuple-element.87.refs_2_, f32[1,2704,256]{2,1,0:T(8,128)} %get-tuple-element.88.refs_3_, f32[64,1184]{1,0:T(8,128)} %bitcast.60, ...), custom_call_target="tpu_custom_call" | custom-call | flops 20000000000 | bytes 20000000 | tf_op jit(solution)/shard_map/pallas_call | solution.py:756
  209.0 7.6 %all-to-all-done.5.refs_1_ = bf16[8,3,56,128]{3,2,1,0:T(8,128)(2,1)S(1)} async-done(((bf16[8,3,56,128]{3,2,1,0:T(8,128)(2,1)}), bf16[8,3,56,128]{3,2,1,0:T(8,128)(2,1)S(1)}, u32[]{:S(2)}, u32[]{:S(2)}) %all-to-all-start.5) | async-done | bytes 344096 | tf_op jit(solution)/shard_map/all_to_all | solution.py:776
  217.3 31.5 %shard_map.369 = (f32[3,832,64]{2,1,0:T(8,128)}, bf16[8,3,56,128]{3,2,1,0:T(8,128)(2,1)}, f32[1696,128]{1,0:T(8,128)}) custom-call(f32[3,832,64]{2,1,0:T(8,128)} %get-tuple-element.85.refs_0_, bf16[8,3,56,128]{3,2,1,0:T(8,128)(2,1)} %copy-done.5, s32[8]{0:T(128)} %refs_2_.5, bf16[3,800,64]{2,1,0:T(8,128)(2,1)} %get-tuple-element.90.refs_3_, ...), custom_call_target="tpu_custom_call" | custom-call | flops 20000000000 | bytes 20000000 | tf_op jit(solution)/shard_map/pallas_call | solution.py:756
  248.8 3.8 all-to-all-start.6
  254.4 6.9 %all-to-all-done.6 = bf16[8,3,56,128]{3,2,1,0:T(8,128)(2,1)S(1)} async-done(((bf16[8,3,56,128]{3,2,1,0:T(8,128)(2,1)}), bf16[8,3,56,128]{3,2,1,0:T(8,128)(2,1)S(1)}, u32[]{:S(2)}, u32[]{:S(2)}) %all-to-all-start.6) | async-done | bytes 344096 | tf_op jit(solution)/shard_map/all_to_all | solution.py:776
  262.1 22.5 %shard_map.370 = (bf16[24,56,128]{2,1,0:T(8,128)(2,1)}, f32[1696,128]{1,0:T(8,128)}) custom-call(bf16[24,56,128]{2,1,0:T(8,128)(2,1)} %bitcast.47, bf16[24,56,128]{2,1,0:T(8,128)(2,1)} %bitcast.46, f32[1,2704,256]{2,1,0:T(8,128)} %get-tuple-element.95.refs_2_, f32[1,2704,256]{2,1,0:T(8,128)} %get-tuple-element.96.refs_3_, f32[64,1184]{1,0:T(8,128)} %bitcast.62, ...), custom_call_target="tpu_custom_call" | custom-call | flops 20000000000 | bytes 20000000 | tf_op jit(solution)/shard_map/pallas_call | solution.py:756
  284.5 4.2 all-to-all-start.7
  292.9 4.7 %all-to-all-done.7.refs_1_ = bf16[8,3,56,128]{3,2,1,0:T(8,128)(2,1)} async-done(((bf16[8,3,56,128]{3,2,1,0:T(8,128)(2,1)}), bf16[8,3,56,128]{3,2,1,0:T(8,128)(2,1)}, u32[]{:S(2)}, u32[]{:S(2)}) %all-to-all-start.7) | async-done | bytes 344096 | tf_op jit(solution)/shard_map/all_to_all | solution.py:776
  301.0 34.5 %shard_map.371 = f32[1856,128]{1,0:T(8,128)} custom-call(f32[3,832,64]{2,1,0:T(8,128)} %get-tuple-element.93.refs_0_, bf16[8,3,56,128]{3,2,1,0:T(8,128)(2,1)} %all-to-all-done.7.refs_1_, s32[8]{0:T(128)} %refs_2_.5, bf16[3,800,64]{2,1,0:T(8,128)(2,1)} %get-tuple-element.98.refs_3_, f32[3,816,256]{2,1,0:T(8,128)} %get-tuple-element.99.refs_4_, ...), custom_call_target="tpu_custom_call" | custom-call | flops 20000000000 | bytes 20000000 | tf_op jit(solution)/shard_map/pallas_call | solution.py:756
  340.1 5.9 %all-to-all-start.11 = ((f32[8,56,128]{2,1,0:T(8,128)}), f32[8,56,128]{2,1,0:T(8,128)S(1)}, u32[]{:S(2)}, u32[]{:S(2)}) async-start(f32[8,56,128]{2,1,0:T(8,128)} %bitcast.16), calls=%async_computation.11 | async-start | bytes 458752 | tf_op jit(solution)/shard_map/all_to_all | solution.py:776
  348.5 6.3 %all-to-all-done.11 = f32[8,56,128]{2,1,0:T(8,128)S(1)} async-done(((f32[8,56,128]{2,1,0:T(8,128)}), f32[8,56,128]{2,1,0:T(8,128)S(1)}, u32[]{:S(2)}, u32[]{:S(2)}) %all-to-all-start.11) | async-done | bytes 229408 | tf_op jit(solution)/shard_map/all_to_all | solution.py:776
  359.0 7.3 %all-to-all-done.9 = f32[8,56,128]{2,1,0:T(8,128)S(1)} async-done(((f32[8,56,128]{2,1,0:T(8,128)}), f32[8,56,128]{2,1,0:T(8,128)S(1)}, u32[]{:S(2)}, u32[]{:S(2)}) %all-to-all-start.9) | async-done | bytes 229408 | tf_op jit(solution)/shard_map/all_to_all | solution.py:776
  369.8 8.4 %all-to-all-done.8 = f32[8,64,128]{2,1,0:T(8,128)S(1)} async-done(((f32[8,64,128]{2,1,0:T(8,128)}), f32[8,64,128]{2,1,0:T(8,128)S(1)}, u32[]{:S(2)}, u32[]{:S(2)}) %all-to-all-start.8) | async-done | bytes 262176 | tf_op jit(solution)/shard_map/all_to_all | solution.py:776
  379.0 3.6 all-to-all-start.13
  382.7 12.6 %all-to-all-done.13 = f32[8,112,128]{2,1,0:T(8,128)S(1)} async-done(((f32[8,112,128]{2,1,0:T(8,128)}), f32[8,112,128]{2,1,0:T(8,128)S(1)}, u32[]{:S(2)}, u32[]{:S(2)}) %all-to-all-start.13) | async-done | bytes 458784 | tf_op jit(solution)/shard_map/all_to_all | solution.py:776
  396.0 3.9 all-to-all-start.10
  402.2 6.2 %collective-permute-done.18 = f32[424,128]{1,0:T(8,128)S(1)} collective-permute-done((f32[424,128]{1,0:T(8,128)S(1)}, f32[424,128]{1,0:T(8,128)S(1)}, u32[]{:S(2)}, u32[]{:S(2)}) %collective-permute-start.18) | collective-permute-done | bytes 217120 | tf_op jit(solution)/shard_map/ppermute | solution.py:781
  408.5 4.6 %all-to-all-done.10 = f32[8,120,128]{2,1,0:T(8,128)S(1)} async-done(((f32[8,120,128]{2,1,0:T(8,128)}), f32[8,120,128]{2,1,0:T(8,128)S(1)}, u32[]{:S(2)}, u32[]{:S(2)}) %all-to-all-start.10) | async-done | bytes 491552 | tf_op jit(solution)/shard_map/all_to_all | solution.py:776
  415.5 5.6 %collective-permute-done.10 = f32[424,128]{1,0:T(8,128)S(1)} collective-permute-done((f32[424,128]{1,0:T(8,128)S(1)}, f32[424,128]{1,0:T(8,128)S(1)}, u32[]{:S(2)}, u32[]{:S(2)}) %collective-permute-start.10) | collective-permute-done | bytes 217120 | tf_op jit(solution)/shard_map/ppermute | solution.py:781
  427.3 14.6 %shard_map.372 = (f32[8,128]{1,0:T(8,128)}, f32[4,2,64,512]{3,2,1,0:T(8,128)}, f32[4,2,128,512]{3,2,1,0:T(8,128)}, f32[64,1184]{1,0:T(8,128)}, f32[40,128]{1,0:T...) custom-call(f32[1856,128]{1,0:T(8,128)} %maximum_select_fusion.refs_, ...), custom_call_target="tpu_custom_call" | custom-call | flops 20000000000 | bytes 20000000 | tf_op jit(solution)/shard_map/pallas_call | solution.py:756
  (110 shorter events, 57.6 us)
Async XLA Ops:
  2.1 8.9 %collective-permute-start = (f32[2,8,416]{2,1,0:T(8,128)S(1)}, f32[2,8,416]{2,1,0:T(8,128)S(1)}, u32[]{:S(2)}, u32[]{:S(2)}) collective-permute-start(f32[2,8,416]{2,1,0:T(8,128)S(1)} %pad_maximum_fusion.2), channel_id=1, source_target_pairs={{4,0},{8,4},{12,8},{16,12},{20,16},{24,20},{28,24},{5,1},{9,5},{13... | collective-permute-start | bytes 79880 | tf_op jit(solution)/shard_map/ppermute | solution.py:772
  4.2 6.8 %collective-permute-start.1 = (f32[8,8]{1,0:T(8,128)S(1)}, f32[8,8]{1,0:T(8,128)S(1)}, u32[]{:S(2)}, u32[]{:S(2)}) collective-permute-start(f32[8,8]{1,0:T(8,128)S(1)} %slice.44), channel_id=1, source_target_pairs={{0,4},{4,8},{8,12},{12,16},{16,20},{20,24},{24,28},{1,5},{5,9},{9,... | collective-permute-start | bytes 776 | tf_op jit(solution)/shard_map/ppermute | solution.py:772
  152.4 5.2 %collective-permute-start.2 = (f32[208,128]{1,0:T(8,128)}, f32[208,128]{1,0:T(8,128)S(1)}, u32[]{:S(2)}, u32[]{:S(2)}) collective-permute-start(f32[208,128]{1,0:T(8,128)} %get-tuple-element.82), channel_id=1, source_target_pairs={{0,4},{4,8},{8,12},{12,16},{16,20},{20,24},{24,28},{1,5},{5,9},{9,... | collective-permute-start | bytes 319496 | tf_op jit(solution)/shard_map/ppermute | solution.py:772
  155.0 6.8 %collective-permute-start.3 = (f32[208,128]{1,0:T(8,128)}, f32[208,128]{1,0:T(8,128)S(1)}, u32[]{:S(2)}, u32[]{:S(2)}) collective-permute-start(f32[208,128]{1,0:T(8,128)} %get-tuple-element.83), channel_id=1, source_target_pairs={{4,0},{8,4},{12,8},{16,12},{20,16},{24,20},{28,24},{5,1},{9,5},{13... | collective-permute-start | bytes 319496 | tf_op jit(solution)/shard_map/ppermute | solution.py:772
  204.4 12.2 %all-to-all-start.5 = ((bf16[8,3,56,128]{3,2,1,0:T(8,128)(2,1)}), bf16[8,3,56,128]{3,2,1,0:T(8,128)(2,1)S(1)}, u32[]{:S(2)}, u32[]{:S(2)}) async-start(bf16[8,3,56,128]{3,2,1,0:T(8,128)(2,1)} %bitcast.51), calls=%async_computation.5 | async-start | bytes 688128 | tf_op jit(solution)/shard_map/all_to_all | solution.py:776
  208.9 43.7 %collective-permute-start.14 = (f32[848,128]{1,0:T(8,128)S(1)}, f32[848,128]{1,0:T(8,128)S(1)}, u32[]{:S(2)}, u32[]{:S(2)}) collective-permute-start(f32[848,128]{1,0:T(8,128)S(1)} %constant_dynamic-slice_fusion.1), channel_id=1, source_target_pairs={{0,1},{1,0},{2,3},{3,2},{4,5},{5,4},{6,7},{7,6},{8,9},{9,8},{10,11... | collective-permute-start | bytes 1302536 | tf_op jit(solution)/shard_map/ppermute | solution.py:781
  217.3 35.4 %copy-start.2 = (f32[1696,128]{1,0:T(8,128)S(1)}, f32[1696,128]{1,0:T(8,128)}, u32[]{:S(2)}) copy-start(f32[1696,128]{1,0:T(8,128)} %get-tuple-element.105) | copy-start | bytes 2605060
  248.8 12.5 %all-to-all-start.6 = ((bf16[8,3,56,128]{3,2,1,0:T(8,128)(2,1)}), bf16[8,3,56,128]{3,2,1,0:T(8,128)(2,1)S(1)}, u32[]{:S(2)}, u32[]{:S(2)}) async-start(bf16[8,3,56,128]{3,2,1,0:T(8,128)(2,1)} %get-tuple-element.94), calls=%async_computation.6 | async-start | bytes 688128 | tf_op jit(solution)/shard_map/all_to_all | solution.py:776
  252.7 36.0 %collective-permute-start.15 = (f32[424,128]{1,0:T(8,128)S(1)}, f32[424,128]{1,0:T(8,128)}, u32[]{:S(2)}, u32[]{:S(2)}) collective-permute-start(f32[424,128]{1,0:T(8,128)S(1)} %constant_dynamic-slice_fusion), channel_id=1, source_target_pairs={{0,2},{1,3},{2,0},{3,1},{4,6},{5,7},{6,4},{7,5},{8,10},{9,11},{10,... | collective-permute-start | bytes 651272 | tf_op jit(solution)/shard_map/ppermute | solution.py:781
  254.3 36.1 %collective-permute-start.12 = (f32[848,128]{1,0:T(8,128)S(1)}, f32[848,128]{1,0:T(8,128)S(1)}, u32[]{:S(2)}, u32[]{:S(2)}) collective-permute-start(f32[848,128]{1,0:T(8,128)S(1)} %constant_dynamic-slice_fusion.3), channel_id=1, source_target_pairs={{0,1},{1,0},{2,3},{3,2},{4,5},{5,4},{6,7},{7,6},{8,9},{9,8},{10,11... | collective-permute-start | bytes 1302536 | tf_op jit(solution)/shard_map/ppermute | solution.py:781
  284.5 7.6 %copy-start.3 = (f32[1696,128]{1,0:T(8,128)S(1)}, f32[1696,128]{1,0:T(8,128)}, u32[]{:S(2)}) copy-start(f32[1696,128]{1,0:T(8,128)} %get-tuple-element.103) | copy-start | bytes 2605060
  284.5 13.0 %all-to-all-start.7 = ((bf16[8,3,56,128]{3,2,1,0:T(8,128)(2,1)}), bf16[8,3,56,128]{3,2,1,0:T(8,128)(2,1)}, u32[]{:S(2)}, u32[]{:S(2)}) async-start(bf16[8,3,56,128]{3,2,1,0:T(8,128)(2,1)} %bitcast.50), calls=%async_computation.7 | async-start | bytes 688128 | tf_op jit(solution)/shard_map/all_to_all | solution.py:776
  290.5 46.2 %collective-permute-start.13 = (f32[424,128]{1,0:T(8,128)S(1)}, f32[424,128]{1,0:T(8,128)S(1)}, u32[]{:S(2)}, u32[]{:S(2)}) collective-permute-start(f32[424,128]{1,0:T(8,128)S(1)} %constant_dynamic-slice_fusion.2), channel_id=1, source_target_pairs={{0,2},{1,3},{2,0},{3,1},{4,6},{5,7},{6,4},{7,5},{8,10},{9,11},{10,... | collective-permute-start | bytes 651272 | tf_op jit(solution)/shard_map/ppermute | solution.py:781
  292.9 44.6 %collective-permute-start.6 = (f32[848,128]{1,0:T(8,128)}, f32[848,128]{1,0:T(8,128)}, u32[]{:S(2)}, u32[]{:S(2)}) collective-permute-start(f32[848,128]{1,0:T(8,128)} %constant_dynamic-slice_fusion.5), channel_id=1, source_target_pairs={{0,1},{1,0},{2,3},{3,2},{4,5},{5,4},{6,7},{7,6},{8,9},{9,8},{10,11... | collective-permute-start | bytes 1302536 | tf_op jit(solution)/shard_map/ppermute | solution.py:781
  297.6 42.5 %all-to-all-start.12 = ((f32[8,56,128]{2,1,0:T(8,128)}), f32[8,56,128]{2,1,0:T(8,128)S(1)}, u32[]{:S(2)}, u32[]{:S(2)}) async-start(f32[8,56,128]{2,1,0:T(8,128)} %bitcast.17), calls=%async_computation.12 | async-start | bytes 458752 | tf_op jit(solution)/shard_map/all_to_all | solution.py:776
  335.5 10.6 %copy-start = (f32[1856,128]{1,0:T(8,128)S(1)}, f32[1856,128]{1,0:T(8,128)}, u32[]{:S(2)}) copy-start(f32[1856,128]{1,0:T(8,128)} %shard_map.371) | copy-start | bytes 2850820
  336.6 9.4 %collective-permute-start.4 = (f32[928,128]{1,0:T(8,128)S(1)}, f32[928,128]{1,0:T(8,128)}, u32[]{:S(2)}, u32[]{:S(2)}) collective-permute-start(f32[928,128]{1,0:T(8,128)S(1)} %constant_dynamic-slice_fusion.7), channel_id=1, source_target_pairs={{0,1},{1,0},{2,3},{3,2},{4,5},{5,4},{6,7},{7,6},{8,9},{9,8},{10,11... | collective-permute-start | bytes 1425416 | tf_op jit(solution)/shard_map/ppermute | solution.py:781
  338.6 9.2 %collective-permute-start.7 = (f32[424,128]{1,0:T(8,128)S(1)}, f32[424,128]{1,0:T(8,128)S(1)}, u32[]{:S(2)}, u32[]{:S(2)}) collective-permute-start(f32[424,128]{1,0:T(8,128)S(1)} %constant_dynamic-slice_fusion.4), channel_id=1, source_target_pairs={{0,2},{1,3},{2,0},{3,1},{4,6},{5,7},{6,4},{7,5},{8,10},{9,11},{10,... | collective-permute-start | bytes 651272 | tf_op jit(solution)/shard_map/ppermute | solution.py:781
  340.1 14.7 %all-to-all-start.11 = ((f32[8,56,128]{2,1,0:T(8,128)}), f32[8,56,128]{2,1,0:T(8,128)S(1)}, u32[]{:S(2)}, u32[]{:S(2)}) async-start(f32[8,56,128]{2,1,0:T(8,128)} %bitcast.16), calls=%async_computation.11 | async-start | bytes 458752 | tf_op jit(solution)/shard_map/all_to_all | solution.py:776
  347.2 11.1 %collective-permute-start.5 = (f32[464,128]{1,0:T(8,128)S(1)}, f32[464,128]{1,0:T(8,128)S(1)}, u32[]{:S(2)}, u32[]{:S(2)}) collective-permute-start(f32[464,128]{1,0:T(8,128)S(1)} %constant_dynamic-slice_fusion.6), channel_id=1, source_target_pairs={{0,2},{1,3},{2,0},{3,1},{4,6},{5,7},{6,4},{7,5},{8,10},{9,11},{10,... | collective-permute-start | bytes 712712 | tf_op jit(solution)/shard_map/ppermute | solution.py:781
  354.8 11.5 %all-to-all-start.9 = ((f32[8,56,128]{2,1,0:T(8,128)}), f32[8,56,128]{2,1,0:T(8,128)S(1)}, u32[]{:S(2)}, u32[]{:S(2)}) async-start(f32[8,56,128]{2,1,0:T(8,128)} %bitcast.13), calls=%async_computation.9 | async-start | bytes 458752 | tf_op jit(solution)/shard_map/all_to_all | solution.py:776
  366.3 11.9 %all-to-all-start.8 = ((f32[8,64,128]{2,1,0:T(8,128)}), f32[8,64,128]{2,1,0:T(8,128)S(1)}, u32[]{:S(2)}, u32[]{:S(2)}) async-start(f32[8,64,128]{2,1,0:T(8,128)} %bitcast.12), calls=%async_computation.8 | async-start | bytes 524288 | tf_op jit(solution)/shard_map/all_to_all | solution.py:776
  379.0 16.2 %all-to-all-start.13 = ((f32[8,112,128]{2,1,0:T(8,128)}), f32[8,112,128]{2,1,0:T(8,128)S(1)}, u32[]{:S(2)}, u32[]{:S(2)}) async-start(f32[8,112,128]{2,1,0:T(8,128)} %broadcast_in_dim.5), calls=%async_computation.13 | async-start | bytes 917504 | tf_op jit(solution)/shard_map/all_to_all | solution.py:776
  396.0 17.0 %all-to-all-start.10 = ((f32[8,120,128]{2,1,0:T(8,128)}), f32[8,120,128]{2,1,0:T(8,128)S(1)}, u32[]{:S(2)}, u32[]{:S(2)}) async-start(f32[8,120,128]{2,1,0:T(8,128)} %broadcast_in_dim.4), calls=%async_computation.10 | async-start | bytes 983040 | tf_op jit(solution)/shard_map/all_to_all | solution.py:776
  400.0 8.3 %collective-permute-start.18 = (f32[424,128]{1,0:T(8,128)S(1)}, f32[424,128]{1,0:T(8,128)S(1)}, u32[]{:S(2)}, u32[]{:S(2)}) collective-permute-start(f32[424,128]{1,0:T(8,128)S(1)} %slice.63), channel_id=1, source_target_pairs={{0,2},{1,3},{2,0},{3,1},{4,6},{5,7},{6,4},{7,5},{8,10},{9,11},{10,... | collective-permute-start | bytes 651272 | tf_op jit(solution)/shard_map/ppermute | solution.py:781
  400.7 13.1 %collective-permute-start.16 = (f32[424,128]{1,0:T(8,128)S(1)}, f32[424,128]{1,0:T(8,128)S(1)}, u32[]{:S(2)}, u32[]{:S(2)}) collective-permute-start(f32[424,128]{1,0:T(8,128)S(1)} %slice.61), channel_id=1, source_target_pairs={{0,2},{1,3},{2,0},{3,1},{4,6},{5,7},{6,4},{7,5},{8,10},{9,11},{10,... | collective-permute-start | bytes 651272 | tf_op jit(solution)/shard_map/ppermute | solution.py:781
  408.4 12.8 %collective-permute-start.19 = (f32[848,128]{1,0:T(8,128)S(1)}, f32[848,128]{1,0:T(8,128)S(1)}, u32[]{:S(2)}, u32[]{:S(2)}) collective-permute-start(f32[848,128]{1,0:T(8,128)S(1)} %maximum_select_fusion.7), channel_id=1, source_target_pairs={{0,1},{1,0},{2,3},{3,2},{4,5},{5,4},{6,7},{7,6},{8,9},{9,8},{10,11... | collective-permute-start | bytes 1302536 | tf_op jit(solution)/shard_map/ppermute | solution.py:781
  413.1 8.0 %collective-permute-start.10 = (f32[424,128]{1,0:T(8,128)S(1)}, f32[424,128]{1,0:T(8,128)S(1)}, u32[]{:S(2)}, u32[]{:S(2)}) collective-permute-start(f32[424,128]{1,0:T(8,128)S(1)} %slice.59), channel_id=1, source_target_pairs={{0,2},{1,3},{2,0},{3,1},{4,6},{5,7},{6,4},{7,5},{8,10},{9,11},{10,... | collective-permute-start | bytes 651272 | tf_op jit(solution)/shard_map/ppermute | solution.py:781
  413.8 10.5 %collective-permute-start.17 = (f32[848,128]{1,0:T(8,128)S(1)}, f32[848,128]{1,0:T(8,128)S(1)}, u32[]{:S(2)}, u32[]{:S(2)}) collective-permute-start(f32[848,128]{1,0:T(8,128)S(1)} %maximum_select_fusion.6), channel_id=1, source_target_pairs={{0,1},{1,0},{2,3},{3,2},{4,5},{5,4},{6,7},{7,6},{8,9},{9,8},{10,11... | collective-permute-start | bytes 1302536 | tf_op jit(solution)/shard_map/ppermute | solution.py:781
  413.9 10.3 %collective-permute-start.8 = (f32[464,128]{1,0:T(8,128)S(1)}, f32[464,128]{1,0:T(8,128)S(1)}, u32[]{:S(2)}, u32[]{:S(2)}) collective-permute-start(f32[464,128]{1,0:T(8,128)S(1)} %slice.57), channel_id=1, source_target_pairs={{0,2},{1,3},{2,0},{3,1},{4,6},{5,7},{6,4},{7,5},{8,10},{9,11},{10,... | collective-permute-start | bytes 712712 | tf_op jit(solution)/shard_map/ppermute | solution.py:781
  421.1 4.2 collective-permute-start.11
  424.2 2.0 collective-permute-start.9
  (7 other events, 13.0 us)
